TPU v7x, 32 devices: a whole 2x2x4 slice. The times are simulated.
32 devices in a mesh: pair: 4 (over x, core), grow: 2 (over y), gcol: 4 (over z).
Axes of the slice: x: 2, y: 2, z: 4, core: 2. Of those that a mesh axis runs over, the one named last changes fastest.
Arguments:
- valence: bfloat16 [48, 32768], replicated, may hold values from -6 to 6
- conduction: bfloat16 [64, 32768], P('pair'), may hold values from -6 to 6
- valence_energy: float32 [48], replicated, may hold values from -12 to -1
- conduction_energy: float32 [64], P('pair'), may hold values from 0.5 to 8
- pair_valence: int32 [64], P(('pair', 'grow', 'gcol')), may hold values from 0 to 47
- pair_conduction: int32 [64], P(('pair', 'grow', 'gcol')), may hold values from 0 to 15
- pair_count: int32 [32], P(('pair', 'grow', 'gcol')), may hold values from 1 to 2, as said below
- g_index: int32 [9216], replicated, may hold values from 1 to 32767, as said below
Outputs:
- chi: float32 [9216, 9216], P(('pair', 'grow'), 'gcol')
Inputs may be any that keep to these rules, and one draw needn't show every extreme that they name: `pair_count`: every device has at least one live slot, and some device has exactly 2. `g_index`: distinct cells; with centred frequencies (an index v stands for v - 32 when v >= 16) they are the 9216 cells of smallest |G| other than G = 0 and the planes at frequency -16, closed under G -> -G, in no particular order.
All inputs are finite; a program needn't handle non-finite values.
Results may differ from a plain program's by a relative error of at most 0.0037.
Values may be sent and summed in bfloat16 or wider, within the bound.
A program may use at most 128 MiB of HBM per device.

v0:
```python
import math

import jax
import jax.numpy as jnp
from jax import lax
from jax.sharding import PartitionSpec as P

GRID = 32


def dft_tables(length):
    points = jnp.arange(length, dtype=jnp.int32)
    phases = points[:, None] * points[None, :] % length
    angles = phases.astype(jnp.float32) * (2.0 * math.pi / length)
    return (jnp.cos(angles), jnp.sin(angles))


def transform(density):
    cosine_table, sine_table = dft_tables(density.shape[-1])
    highest = lax.Precision.HIGHEST
    real_part = jnp.einsum("pabn,nk->pabk", density, cosine_table, precision=highest)
    imag_part = -jnp.einsum("pabn,nk->pabk", density, sine_table, precision=highest)
    real_next = jnp.einsum(
        "panc,nk->pakc", real_part, cosine_table, precision=highest
    ) + jnp.einsum("panc,nk->pakc", imag_part, sine_table, precision=highest)
    imag_next = jnp.einsum(
        "panc,nk->pakc", imag_part, cosine_table, precision=highest
    ) - jnp.einsum("panc,nk->pakc", real_part, sine_table, precision=highest)
    real_last = jnp.einsum(
        "pnbc,nk->pkbc", real_next, cosine_table, precision=highest
    ) + jnp.einsum("pnbc,nk->pkbc", imag_next, sine_table, precision=highest)
    imag_last = jnp.einsum(
        "pnbc,nk->pkbc", imag_next, cosine_table, precision=highest
    ) - jnp.einsum("pnbc,nk->pkbc", real_next, sine_table, precision=highest)
    return (real_last, imag_last)


def local(
    valence,
    conduction,
    valence_energy,
    conduction_energy,
    pair_valence,
    pair_conduction,
    pair_count,
    g_index,
):
    slot_count = pair_valence.shape[0]
    total_g = g_index.shape[0]
    n_pair = lax.axis_size("pair")
    n_grow = lax.axis_size("grow")
    n_gcol = lax.axis_size("gcol")
    phi_valence = jnp.take(valence, pair_valence, axis=0).astype(jnp.float32)
    phi_conduction = jnp.take(conduction, pair_conduction, axis=0).astype(jnp.float32)
    density = (phi_valence * phi_conduction).reshape(slot_count, GRID, GRID, GRID)
    real_grid, imag_grid = transform(density)
    real_sel = jnp.take(real_grid.reshape(slot_count, -1), g_index, axis=1)
    imag_sel = jnp.take(imag_grid.reshape(slot_count, -1), g_index, axis=1)
    valence_pick = (
        pair_valence[:, None] == jnp.arange(valence_energy.shape[0], dtype=jnp.int32)[None, :]
    ).astype(jnp.float32)
    conduction_pick = (
        pair_conduction[:, None] == jnp.arange(conduction_energy.shape[0], dtype=jnp.int32)[None, :]
    ).astype(jnp.float32)
    energy_gap = jnp.sum(conduction_pick * conduction_energy[None, :], axis=1) - jnp.sum(
        valence_pick * valence_energy[None, :], axis=1
    )
    live_slots = (jnp.arange(slot_count, dtype=jnp.int32) < pair_count[0]).astype(jnp.float32)
    factor = live_slots * jnp.sqrt(4.0 / energy_gap) / jnp.sqrt(jnp.float32(GRID**3))
    amplitudes = jnp.concatenate(
        [real_sel * factor[:, None], imag_sel * factor[:, None]], axis=0
    ).astype(jnp.bfloat16)
    doubled = amplitudes.shape[0]
    sub_rows = total_g // (n_pair * n_grow)
    col_width = total_g // n_gcol
    by_rows = amplitudes.reshape(doubled, n_pair, n_grow, sub_rows)
    row_panel = lax.all_to_all(by_rows, "grow", split_axis=2, concat_axis=0, tiled=True)
    row_panel = row_panel.reshape(1, n_grow, doubled, n_pair * sub_rows)
    by_columns = amplitudes.reshape(doubled, n_gcol, col_width)
    col_panel = lax.all_to_all(by_columns, "gcol", split_axis=1, concat_axis=0, tiled=True)
    col_panel = lax.all_gather(
        col_panel.reshape(1, n_gcol, doubled, col_width), "grow", axis=0, tiled=True
    )
    all_rows = lax.all_gather(row_panel, "gcol", axis=0, tiled=True)
    partial_value = jnp.einsum(
        "crsa,rcsb->ab", all_rows, col_panel, preferred_element_type=jnp.float32
    )
    summed = lax.psum_scatter(partial_value, "pair", scatter_dimension=0, tiled=True)
    total_slots = slot_count * n_pair * n_grow * n_gcol
    return -summed / jnp.sqrt(jnp.float32(total_slots))


def solution(mesh):
    return jax.shard_map(
        local,
        mesh=mesh,
        in_specs=(
            P(),
            P("pair", None),
            P(),
            P("pair"),
            P(("pair", "grow", "gcol")),
            P(("pair", "grow", "gcol")),
            P(("pair", "grow", "gcol")),
            P(),
        ),
        out_specs=P(("pair", "grow"), "gcol"),
        check_vma=False,
    )
```

profile of v0, /device:TPU:0, one launch (start us, length us, event | category | flops | bytes accessed | tf_op | source)
XLA Modules:
  0.0 495.0 jit_solution(16010935355955792271)
XLA Ops:
  6.5 0.0 copy-start
  6.5 0.8 compare_select_fusion.2
  7.4 0.9 compare_select_fusion.1
  8.2 0.7 compare_and_fusion.1
  8.9 0.8 compare_and_fusion
  9.7 0.8 fusion.14
  10.5 2.2 gather_fusion.1
  12.7 1.0 gather.18
  13.7 0.0 copy-done
  13.7 0.7 gather_fusion
  14.5 0.3 gather.16
  14.7 2.2 convolution_negate_fusion
  16.9 2.2 fusion.6
  19.7 0.0 copy-done.2
  19.7 0.0 copy-done.4
  19.8 0.2 fusion.46
  19.9 0.0 copy-done.3
  19.9 0.2 fusion.45
  20.1 1.1 fusion.28
  21.2 1.1 fusion.25
  22.3 1.1 fusion.5
  23.4 1.1 fusion.4
  24.5 1.6 fusion.7
  26.1 1.6 fusion.11
  27.7 1.8 fusion.2
  29.5 1.6 fusion.3
  31.1 9.2 %copy.84 = f32[2,32,32,32]{0,3,2,1:T(8,128)} copy(f32[2,32,32,32]{3,1,2,0:T(8,128)S(1)} %fusion.3) | data formatting | bytes 524288 | tf_op jit(solution)/shard_map/reshape | solution.py:57
  40.3 9.2 %copy.85 = f32[2,32,32,32]{0,3,2,1:T(8,128)} copy(f32[2,32,32,32]{3,1,2,0:T(8,128)S(1)} %fusion.2) | data formatting | bytes 524288 | tf_op jit(solution)/shard_map/reshape | solution.py:58
  49.5 37.0 %gather_fusion.2 = f32[9216,2]{1,0:T(8,128)} fusion(f32[2,32768]{0,1:T(8,128)} %bitcast.75, s32[9216]{0:T(1024)S(1)} %fusion.14), kind=kCustom, calls=%fused_computation.clone | custom fusion | bytes 184320 | tf_op jit(solution)/shard_map/jit(_take)/gather | solution.py:57
  86.5 37.0 %gather_fusion.3 = f32[9216,2]{1,0:T(8,128)} fusion(f32[2,32768]{0,1:T(8,128)} %bitcast.74, s32[9216]{0:T(1024)S(1)} %fusion.14), kind=kCustom, calls=%fused_computation.1.clone | custom fusion | bytes 184320 | tf_op jit(solution)/shard_map/jit(_take)/gather | solution.py:58
  123.5 8.4 %fusion.1 = (bf16[2,9216]{0,1:T(8,128)(2,1)S(1)}, bf16[2,9216]{0,1:T(8,128)(2,1)}) fusion(f32[9216,2]{1,0:T(8,128)} %gather_fusion.2, f32[2]{0:T(128)S(1)} %fusion.47, pred[9216]{0:T(1024)(128)(4,1)S(1)} %compare_and_fusion, f32[9216,2]{1,0:T(8,128)} %gather_fusion.3), kind=kLoop, calls=%fused_computation.9 | loop fusion | flops 110592 | bytes 230408 | tf_op jit(solution)/shard_map/convert.7
  131.8 2.1 copy.73
  134.0 1.0 copy.72
  135.0 0.7 pad_maximum_fusion
  135.7 4.2 all-to-all-start
  139.9 2.1 copy.75
  142.0 1.0 copy.74
  143.1 0.7 pad_maximum_fusion.1
  143.8 0.3 all-to-all-done
  144.1 5.4 %all-to-all-start.1 = ((bf16[4,4,2304]{2,0,1:T(4,128)(2,1)}), bf16[4,4,2304]{2,0,1:T(4,128)(2,1)S(1)}, u32[]{:S(2)}, u32[]{:S(2)}) async-start(bf16[4,4,2304]{2,0,1:T(4,128)(2,1)} %pad_maximum_fusion.1), calls=%async_computation.1 | async-start | bytes 147456 | tf_op jit(solution)/shard_map/all_to_all | solution.py:80
  149.4 0.0 reduce-scatter.2.cloned.1.call-start
  149.5 14.5 %all_gather.6 = bf16[4,2,4,4608]{3,2,1,0:T(4,128)(2,1)S(1)} all-gather(bf16[1,2,4,4608]{3,2,1,0:T(4,128)(2,1)S(1)} %reshape.71), channel_id=1, replica_groups=mesh['pair'=4,'grow'=2,'gcol'=4] {'gcol'}, dimensions={0}, use_global_device_ids=true | all-gather | bytes 368640 | tf_op jit(solution)/shard_map/all_gather | solution.py:84
  164.0 0.0 all-to-all-done.1
  164.0 5.0 %all-gather = bf16[8,4,1,2304]{3,1,2,0:T(4,128)(2,1)S(1)} all-gather(bf16[4,4,1,2304]{3,1,2,0:T(4,128)(2,1)S(1)} %bitcast.76), channel_id=2, replica_groups=mesh['pair'=4,'grow'=2,'gcol'=4] {'grow'}, dimensions={0}, use_global_device_ids=true | all-gather | bytes 221184 | tf_op jit(solution)/shard_map/all_gather | solution.py:81
  169.0 16.4 %convolution_bitcast_fusion = f32[4608,2304]{1,0:T(8,128)} fusion(bf16[4,2,4,4608]{3,2,1,0:T(4,128)(2,1)S(1)} %all_gather.6, bf16[2,4,4,2304]{3,2,1,0:T(4,128)(2,1)S(1)} %bitcast.78), kind=kOutput, calls=%fused_computation.4 | convolution fusion | flops 679477248 | bytes 42909696 | tf_op jit(solution)/shard_map/crsa,rcsb->ab/dot_general | solution.py:85
  185.4 0.0 reduce-scatter.2.cloned.1.call-update
  185.4 293.7 %reduce-scatter.2.cloned.1.call-done = f32[1152,2304]{1,0:T(8,128)} async-done(((f32[4608,2304]{1,0:T(8,128)}), f32[1152,2304]{1,0:T(8,128)}) %reduce-scatter.2.cloned.1.call-update) | async-done | bytes 10616848 | tf_op jit(solution)/shard_map/reduce_scatter | solution.py:88
  479.1 9.0 %negate_multiply_fusion = f32[1152,2304]{1,0:T(8,128)} fusion(f32[1152,2304]{1,0:T(8,128)} %reduce-scatter.2.cloned.1.call-done), kind=kLoop, calls=%fused_computation.5 | loop fusion | flops 5308416 | bytes 21233664 | tf_op jit(solution)/shard_map/div | solution.py:90
  (11 shorter events, 0.1 us)
Async XLA Ops:
  6.5 7.2 %copy-start = (bf16[48,32768]{1,0:T(8,128)(2,1)S(1)}, bf16[48,32768]{1,0:T(8,128)(2,1)}, u32[]{:S(2)}) copy-start(bf16[48,32768]{1,0:T(8,128)(2,1)} %param.10) | copy-start | bytes 9437188
  6.5 13.2 %copy-start.2 = (s32[2]{0:T(128)S(1)}, s32[2]{0:T(128)}, u32[]{:S(2)}) copy-start(s32[2]{0:T(128)} %param.14) | copy-start | bytes 28
  6.5 13.4 %copy-start.3 = (s32[2]{0:T(128)S(1)}, s32[2]{0:T(128)}, u32[]{:S(2)}) copy-start(s32[2]{0:T(128)} %param.15) | copy-start | bytes 28
  6.5 13.2 %copy-start.4 = (f32[48]{0:T(128)S(1)}, f32[48]{0:T(128)}, u32[]{:S(2)}) copy-start(f32[48]{0:T(128)} %param.12) | copy-start | bytes 580
  6.5 13.4 %copy-start.5 = (f32[16]{0:T(128)S(1)}, f32[16]{0:T(128)}, u32[]{:S(2)}) copy-start(f32[16]{0:T(128)} %param.13) | copy-start | bytes 196
  135.7 8.4 %all-to-all-start = ((bf16[4,4,2,1152]{3,1,0,2:T(4,128)(2,1)}), bf16[4,4,2,1152]{3,1,0,2:T(4,128)(2,1)S(1)}, u32[]{:S(2)}, u32[]{:S(2)}) async-start(bf16[4,4,2,1152]{3,1,0,2:T(4,128)(2,1)} %pad_maximum_fusion), calls=%async_computation | async-start | bytes 147456 | tf_op jit(solution)/shard_map/all_to_all | solution.py:77
  144.1 19.9 %all-to-all-start.1 = ((bf16[4,4,2304]{2,0,1:T(4,128)(2,1)}), bf16[4,4,2304]{2,0,1:T(4,128)(2,1)S(1)}, u32[]{:S(2)}, u32[]{:S(2)}) async-start(bf16[4,4,2304]{2,0,1:T(4,128)(2,1)} %pad_maximum_fusion.1), calls=%async_computation.1 | async-start | bytes 147456 | tf_op jit(solution)/shard_map/all_to_all | solution.py:80
  149.4 329.7 %reduce-scatter.2.cloned.1.call-start = ((), (), s32[]{:S(2)}) async-start(), calls=%async_computation.3 | async-start | bytes 53084160 | tf_op jit(solution)/shard_map/reduce_scatter | solution.py:88
  479.1 9.0 %copy-start.1 = (bf16[48,32768]{1,0:T(8,128)(2,1)S(1)}, bf16[48,32768]{1,0:T(8,128)(2,1)}, u32[]{:S(2)}) copy-start(bf16[48,32768]{1,0:T(8,128)(2,1)} %param.10) | copy-start | bytes 9437188
Sparse Core Ops, SparseCore 0:
  185.6 293.5 reduce-scatter.1
where the time goes:
time: 496 us; the launch traced here: 495 us
  waiting for transfers between devices  294 us (59%)
  local copies, waits for them, and re-layouts  103 us (21%)
  matrix products  31.7 us (6%)
  other arithmetic  23.1 us (5%)
  blocking collectives  19.5 us (4%)
  between operations  14.2 us (3%)
  starting transfers between devices  9.59 us (2%)
    reduce_scatter x1, waiting for transfers between devices, local(): lax.psum_scatter(partial_value, 'pair', scatter_dimension=0, tiled=True)  294 us
    gather x1, local copies, waits for them, and re-layouts, local(): real_sel = jnp.take(real_grid.reshape(slot_count, -1), g_index, axis=1)  37 us
    gather x1, local copies, waits for them, and re-layouts, local(): imag_sel = jnp.take(imag_grid.reshape(slot_count, -1), g_index, axis=1)  37 us
    dot_general x1, matrix products, local(): jnp.einsum('crsa,rcsb->ab', all_rows, col_panel, preferred_element_type=j...  16.4 us
    all_gather x1, blocking collectives, local(): all_rows = lax.all_gather(row_panel, 'gcol', axis=0, tiled=True)  14.5 us
  transfers between devices with their start and end apart: 3, of which 2 were waited for; matrix products, arithmetic and copies ran while one was open for 1% of the time, Pallas kernels for 0%

commit v1 on v0

v1 whole, which is shorter than its diff:
```python
import functools
import math

import jax
import jax.numpy as jnp
import ml_dtypes
import numpy as np
from jax import lax
from jax.experimental import pallas as pl
from jax.experimental.pallas import tpu as pltpu
from jax.sharding import PartitionSpec as P

GRID = 32
CHUNK = 16
LANES = 128
TILE = 256
MAIN = 256
MESH = pl.DeviceIdType.MESH
BF16 = jnp.bfloat16
F32 = jnp.float32


def pad_to(size, unit):
    return -(-size // unit) * unit


def ball(total_g):
    freq = np.arange(-(GRID // 2) + 1, GRID // 2)
    square = freq[:, None, None] ** 2 + freq[None, :, None] ** 2 + freq[None, None, :] ** 2
    return int(np.sort(square.ravel())[total_g])


def split(values):
    high = values.astype(ml_dtypes.bfloat16)
    low = (values - high.astype(np.float64)).astype(ml_dtypes.bfloat16)
    return high, low


def tables(total_g):
    limit = ball(total_g)
    reach = math.isqrt(limit)
    plane = []
    for b in range(0, reach + 1):
        for c in range(-reach, reach + 1):
            if b * b + c * c <= limit and (b > 0 or c >= 0):
                plane.append((b * b + c * c, b, c))
    plane.sort()
    extra = plane[MAIN:]
    short = math.isqrt(limit - extra[0][0]) if extra else -1
    width = pad_to(len(plane), LANES)
    keys = np.full((width,), -1, np.int32)
    bs = np.zeros((width,), np.int64)
    cs = np.zeros((width,), np.int64)
    for at, (_, b, c) in enumerate(plane):
        keys[at] = b * GRID + c + GRID // 2
        bs[at], cs[at] = b, c
    cell = np.arange(GRID * GRID)
    phase = (cell[:, None] // GRID * bs[None] + cell[:, None] % GRID * cs[None]) % GRID
    angle = phase * (2.0 * math.pi / GRID)
    used = keys[None] >= 0
    first = np.concatenate([np.cos(angle) * used, -np.sin(angle) * used], axis=1)
    a = np.arange(-reach, reach + 1)
    angle = (a[:, None] * np.arange(GRID)[None] % GRID) * (2.0 * math.pi / GRID)
    small = np.zeros((len(a), 2, 2, GRID))
    small[:, 0, 0], small[:, 0, 1] = np.cos(angle), np.sin(angle)
    small[:, 1, 0], small[:, 1, 1] = -np.sin(angle), np.cos(angle)
    small = small.reshape(len(a) * 2, 2 * GRID)
    second = np.kron(small, np.eye(CHUNK))
    keys = np.repeat(keys[:, None], TILE, axis=1)
    return reach, short, width, keys, split(first), split(second)


def amplitude_kernel(
    reach, short, width, tiles,
    info, energy_v, energy_c, g_list, valence, conduction, keys,
    first_h, first_l, second_h, second_l,
    out, dens_h, dens_l, next_h, next_l, spec,
):
    n_v, n_c = valence.shape[0], conduction.shape[0]
    plane = GRID * GRID
    pick_v = info[:, 0:1] == lax.broadcasted_iota(jnp.int32, (CHUNK, n_v), 1)
    pick_c = info[:, 1:2] == lax.broadcasted_iota(jnp.int32, (CHUNK, n_c), 1)
    live = info[:, 2:3].astype(F32)
    gap = jnp.sum(jnp.where(pick_c, energy_c[...], 0.0), axis=1, keepdims=True) - jnp.sum(
        jnp.where(pick_v, energy_v[...], 0.0), axis=1, keepdims=True
    )
    factor = live * jnp.sqrt(4.0 / gap) / math.sqrt(GRID**3)
    one_v = jnp.where(pick_v, 1.0, 0.0).astype(BF16)
    one_c = jnp.where(pick_c, 1.0, 0.0).astype(BF16)
    dot = functools.partial(jnp.dot, preferred_element_type=F32)

    for i in range(GRID):
        at = slice(i * plane, (i + 1) * plane)
        dens = dot(one_v, valence[:, at]) * dot(one_c, conduction[:, at])
        high = dens.astype(BF16)
        rows = slice(i * CHUNK, (i + 1) * CHUNK)
        dens_h[rows, :] = high
        dens_l[rows, :] = (dens - high.astype(F32)).astype(BF16)

    half = GRID * CHUNK
    for part in range(2):
        at = slice(part * width, (part + 1) * width)
        value = (
            dot(dens_h[...], first_h[:, at])
            + dot(dens_l[...], first_h[:, at])
            + dot(dens_h[...], first_l[:, at])
        )
        high = value.astype(BF16)
        next_h[part * half:(part + 1) * half, :] = high
        next_l[part * half:(part + 1) * half, :] = (value - high.astype(F32)).astype(BF16)

    value = (
        dot(second_h[...], next_h[...])
        + dot(second_h[...], next_l[...])
        + dot(second_l[...], next_h[...])
    )
    count = 2 * (2 * reach + 1)
    value = value.reshape(count, CHUNK, width) * factor[None]
    spec[...] = value.reshape(count * CHUNK, width).astype(BF16)

    rows = 2 * CHUNK
    low, high = (reach - short) * rows, (reach + short + 1) * rows

    def tile(t, carry):
        at = pl.ds(pl.multiple_of(t * TILE, TILE), TILE)
        cell = g_list[:, at]
        centre = lambda v: jnp.where(v < GRID // 2, v, v - GRID)
        a = centre(cell // (GRID * GRID))
        b = centre(cell // GRID % GRID)
        c = centre(cell % GRID)
        flip = (b < 0) | ((b == 0) & (c < 0))
        a = jnp.where(flip, -a, a)
        b = jnp.where(flip, -b, b)
        c = jnp.where(flip, -c, c)
        key = b * GRID + c + GRID // 2
        hot = jnp.where(keys[...] == key, 1.0, 0.0).astype(BF16)
        picked = dot(spec[:, :MAIN], hot[:MAIN])
        if width > MAIN:
            more = dot(spec[low:high, MAIN:], hot[MAIN:])
        total = jnp.zeros((rows, TILE), F32)
        for n in range(2 * reach + 1):
            value = picked[n * rows:(n + 1) * rows]
            if width > MAIN and low <= n * rows < high:
                value = value + more[n * rows - low:(n + 1) * rows - low]
            total = jnp.where(a == n - reach, value, total)
        imag = total[CHUNK:]
        out[:CHUNK, at] = total[:CHUNK].astype(BF16)
        out[CHUNK:, at] = jnp.where(flip, -imag, imag).astype(BF16)
        return carry

    lax.fori_loop(0, tiles, tile, 0)


def amplitudes(info, energy_v, energy_c, g_list, valence, conduction, total_g):
    reach, short, width, keys, first, second = tables(total_g)
    length = g_list.shape[1]
    chunks = info.shape[0] // CHUNK
    consts = [jnp.asarray(x) for x in (keys, *first, *second)]
    whole = lambda x: pl.BlockSpec(x.shape, lambda n: (0, 0), pipeline_mode=pl.Buffered(1))
    args = [energy_v, energy_c, g_list, valence, conduction, *consts]
    rows = 2 * CHUNK * (2 * reach + 1)
    half = GRID * CHUNK
    return pl.pallas_call(
        functools.partial(amplitude_kernel, reach, short, width, length // TILE),
        grid=(chunks,),
        out_shape=jax.ShapeDtypeStruct((chunks * 2 * CHUNK, length), BF16),
        in_specs=[pl.BlockSpec((CHUNK, info.shape[1]), lambda n: (n, 0))] + [whole(x) for x in args],
        out_specs=pl.BlockSpec((2 * CHUNK, length), lambda n: (n, 0)),
        scratch_shapes=[
            pltpu.VMEM((half, GRID * GRID), BF16),
            pltpu.VMEM((half, GRID * GRID), BF16),
            pltpu.VMEM((2 * half, width), BF16),
            pltpu.VMEM((2 * half, width), BF16),
            pltpu.VMEM((rows, width), BF16),
        ],
        compiler_params=pltpu.CompilerParams(vmem_limit_bytes=56 * 2**20),
    )(info, *args)


def exchange_kernel(n_pair, col_pad, row_pad, amp, cols, rows, send_sem, recv_sem, own_sem):
    me = lax.axis_index("pair")
    barrier = pltpu.get_barrier_semaphore()
    for step in range(1, n_pair):
        other = lax.rem(me + step, n_pair)
        pl.semaphore_signal(barrier, inc=1, device_id={"pair": other}, device_id_type=MESH)
    pl.semaphore_wait(barrier, n_pair - 1)
    copies = []
    for step in range(1, n_pair):
        other = lax.rem(me + step, n_pair)
        block = pl.ds(pl.multiple_of(col_pad + other * row_pad, LANES), row_pad)
        for which, (source, target) in enumerate(
            ((amp.at[:, pl.ds(0, col_pad)], cols), (amp.at[:, block], rows))
        ):
            copy = pltpu.make_async_remote_copy(
                src_ref=source,
                dst_ref=target.at[me],
                send_sem=send_sem.at[which, step],
                recv_sem=recv_sem.at[which, step],
                device_id={"pair": other},
                device_id_type=MESH,
            )
            copy.start()
            copies.append(copy)
    block = pl.ds(pl.multiple_of(col_pad + me * row_pad, LANES), row_pad)
    own = [
        pltpu.make_async_copy(amp.at[:, pl.ds(0, col_pad)], cols.at[me], own_sem.at[0]),
        pltpu.make_async_copy(amp.at[:, block], rows.at[me], own_sem.at[1]),
    ]
    for copy in own:
        copy.start()
    for copy in own + copies:
        copy.wait()


def exchange(amp, n_pair, col_pad, row_pad):
    height = amp.shape[0]
    return pl.pallas_call(
        functools.partial(exchange_kernel, n_pair, col_pad, row_pad),
        out_shape=[
            jax.ShapeDtypeStruct((n_pair, height, col_pad), BF16),
            jax.ShapeDtypeStruct((n_pair, height, row_pad), BF16),
        ],
        in_specs=[pl.BlockSpec(memory_space=pl.ANY)],
        out_specs=[pl.BlockSpec(memory_space=pl.ANY)] * 2,
        scratch_shapes=[
            pltpu.SemaphoreType.DMA((2, n_pair)),
            pltpu.SemaphoreType.DMA((2, n_pair)),
            pltpu.SemaphoreType.DMA((2,)),
        ],
        compiler_params=pltpu.CompilerParams(collective_id=0, has_side_effects=True),
    )(amp)


def product_kernel(scale, rows, cols, out):
    value = lax.dot_general(
        rows[...], cols[...], (((0,), (0,)), ((), ())), preferred_element_type=F32
    )
    out[...] = value[: out.shape[0], : out.shape[1]] * scale


def product(rows, cols, n_rows, n_cols, scale):
    depth, row_pad = rows.shape
    block = LANES if n_rows % LANES == 0 else n_rows
    return pl.pallas_call(
        functools.partial(product_kernel, scale),
        grid=(n_rows // block,),
        out_shape=jax.ShapeDtypeStruct((n_rows, n_cols), F32),
        in_specs=[
            pl.BlockSpec((depth, pad_to(block, LANES)), lambda n: (0, n)),
            pl.BlockSpec(cols.shape, lambda n: (0, 0)),
        ],
        out_specs=pl.BlockSpec((block, n_cols), lambda n: (n, 0)),
        compiler_params=pltpu.CompilerParams(vmem_limit_bytes=48 * 2**20),
    )(rows, cols)


def local(
    valence,
    conduction,
    valence_energy,
    conduction_energy,
    pair_valence,
    pair_conduction,
    pair_count,
    g_index,
):
    slot_count = pair_valence.shape[0]
    total_g = g_index.shape[0]
    n_pair = lax.axis_size("pair")
    n_grow = lax.axis_size("grow")
    n_gcol = lax.axis_size("gcol")
    live = (jnp.arange(slot_count, dtype=jnp.int32) < pair_count[0]).astype(jnp.int32)
    info = jnp.stack([pair_valence, pair_conduction, live], axis=1)
    info = lax.all_gather(info, ("grow", "gcol"), axis=0, tiled=True)
    sub_rows = total_g // (n_pair * n_grow)
    col_width = total_g // n_gcol
    row_pad, col_pad = pad_to(sub_rows, LANES), pad_to(col_width, LANES)
    col_list = lax.dynamic_slice(g_index, (lax.axis_index("gcol") * col_width,), (col_width,))
    row_list = lax.dynamic_index_in_dim(
        g_index.reshape(n_pair, n_grow, sub_rows), lax.axis_index("grow"), 1, keepdims=False
    )
    row_list = jnp.pad(row_list, ((0, 0), (0, row_pad - sub_rows))).reshape(-1)
    g_list = jnp.concatenate([jnp.pad(col_list, (0, col_pad - col_width)), row_list])
    length = g_list.shape[0]
    g_list = jnp.pad(g_list, (0, pad_to(length, TILE) - length))[None, :]
    amp = amplitudes(
        info, valence_energy[None, :], conduction_energy[None, :], g_list, valence, conduction, total_g
    )
    cols, rows = exchange(amp, n_pair, col_pad, row_pad)
    total_slots = slot_count * n_pair * n_grow * n_gcol
    return product(
        rows.reshape(-1, row_pad), cols.reshape(-1, col_pad), sub_rows, col_width,
        -1.0 / math.sqrt(total_slots),
    )


def solution(mesh):
    return jax.shard_map(
        local,
        mesh=mesh,
        in_specs=(
            P(),
            P("pair", None),
            P(),
            P("pair"),
            P(("pair", "grow", "gcol")),
            P(("pair", "grow", "gcol")),
            P(("pair", "grow", "gcol")),
            P(),
        ),
        out_specs=P(("pair", "grow"), "gcol"),
        check_vma=False,
    )
```

time: 496 us -> 70 us (0.14)
  waiting for transfers between devices: 294 us -> 0 us
  local copies, waits for them, and re-layouts: 103 us -> 4.41 us
  Pallas kernels: 0 us -> 40.2 us
  matrix products: 31.7 us -> 0 us
  other arithmetic: 23.1 us -> 0.7 us
  between operations: 14.2 us -> 0.7 us
  starting transfers between devices: 9.59 us -> 0 us
    reduce_scatter x1 -> x0, waiting for transfers between devices: 294 us -> none  [local(): lax.psum_scatter(partial_value, 'pair', scatter_dimension=0, tiled=True)]
    gather x6 -> x0, local copies, waits for them, and re-layouts: 78.2 us -> none  [the longest x1 37 us: local(): real_sel = jnp.take(real_grid.reshape(slot_count, -1), g_index, axis=1)]
    pallas_call x0 -> x3, Pallas kernels: none -> 40.2 us  [the longest x1 21.3 us: amplitudes(): pl.pallas_call(functools.partial(amplitude_kernel, reach, short, width, l...]
    dot_general x11 -> x0, matrix products: 31.7 us -> none  [the longest x1 16.4 us: local(): jnp.einsum('crsa,rcsb->ab', all_rows, col_panel, preferred_element_type=j...]
    reshape x3 -> x2, local copies, waits for them, and re-layouts: 18.4 us -> 0.8 us  [the longest x1 0.79 us: local(): g_index.reshape(n_pair, n_grow, sub_rows)]
    all_to_all x2 -> x0, starting transfers between devices: 9.59 us -> none  [the longest x1 5.36 us: local(): lax.all_to_all(by_columns, 'gcol', split_axis=1, concat_axis=0, tiled=True)]
    div x2 -> x0, other arithmetic: 8.99 us -> none  [the longest x1 8.98 us: local(): return -summed / jnp.sqrt(jnp.float32(total_slots))]
    another operation x1, other arithmetic: 8.39 us -> 0.68 us  [local(): info = jnp.stack([pair_valence, pair_conduction, live], axis=1)]
  transfers between devices with their start and end apart: 3 -> 0, of which waited for: 2 -> 0; matrix products, arithmetic and copies ran while one was open for 1% -> 0% of each run, Pallas kernels for 0% -> 0%
where the time goes in v1:
time: 70 us; the launch traced here: 69.3 us
  Pallas kernels  40.2 us (57%)
  blocking collectives  23.3 us (33%)
  local copies, waits for them, and re-layouts  4.41 us (6%)
    all_gather x1, blocking collectives, local(): info = lax.all_gather(info, ('grow', 'gcol'), axis=0, tiled=True)  23.3 us
    pallas_call x1, Pallas kernels, amplitudes(): pl.pallas_call(functools.partial(amplitude_kernel, reach, short, width, l...  21.3 us
    pallas_call x1, Pallas kernels, exchange(): pl.pallas_call(functools.partial(exchange_kernel, n_pair, col_pad, row_pa...  12 us
    pallas_call x1, Pallas kernels, product(): pl.pallas_call(functools.partial(product_kernel, scale), grid=(n_rows //...  6.88 us
    unnamed x4, local copies, waits for them, and re-layouts  2.02 us

profile of v1, /device:TPU:0, one launch (start us, length us, event | category | flops | bytes accessed | tf_op | source)
XLA Modules:
  0.0 69.3 jit_solution(16859073592949184326)
XLA Ops:
  0.7 0.7 pad_add_fusion.1
  1.3 0.1 copy.20
  1.4 23.3 %all-gather = s32[8,2,3]{2,1,0:T(2,128)} all-gather(s32[1,2,3]{2,1,0:T(2,128)S(1)} %bitcast.13), channel_id=1, replica_groups=mesh['pair'=4,'grow'=2,'gcol'=4] {'grow','gcol'}, dimensions={0}, use_global_device_ids=true | all-gather | bytes 216 | tf_op jit(solution)/shard_map/all_gather | solution.py:274
  24.8 0.8 %dynamic_slice.7 = s32[2304]{0:T(1024)S(1)} dynamic-slice(s32[9216]{0:T(1024)} %param.20, s32[]{:T(128)S(6)} %select_n.7), dynamic_slice_sizes={2304} | dynamic-slice | bytes 18436 | tf_op jit(solution)/shard_map/dynamic_slice | solution.py:278
  25.6 0.8 %reshape.23 = s32[4,2,1152]{2,1,0:T(2,128)S(1)} reshape(s32[9216]{0:T(1024)} %param.20) | data formatting | bytes 73728 | tf_op jit(solution)/shard_map/reshape | solution.py:280
  26.4 0.1 dynamic-slice_reduce_fusion
  26.5 0.6 broadcast_in_dim.11.g_list
  27.1 21.3 %shard_map.127.amp = bf16[32,6912]{1,0:T(8,128)(2,1)} custom-call(s32[16,3]{1,0:T(8,128)} %bitcast.12, f32[1,48]{1,0:T(1,128)} %bitcast.14, f32[1,16]{1,0:T(1,128)} %bitcast.15, s32[1,6912]{1,0:T(1,128)} %broadcast_in_dim.11.g_list, bf16[48,32768]{1,0:T(8,128)(2,1)} %valence.1, bf16[16,32768]{1,0:T(8,128)(2,1)} %conduction.1, ...), custom_call_target="tpu_custom_call" | custom-call | tf_op jit(solution)/shard_map/pallas_call | solution.py:163
  48.4 12.0 %shard_map.128 = (bf16[4,32,2304]{2,1,0:T(8,128)(2,1)}, bf16[4,32,1152]{2,1,0:T(8,128)(2,1)}) custom-call(bf16[32,6912]{1,0:T(8,128)(2,1)} %shard_map.127.amp), custom_call_target="tpu_custom_call" | custom-call | tf_op jit(solution)/shard_map/pallas_call | solution.py:217
  60.4 0.0 copy-start
  60.4 1.1 %copy-done = bf16[4,32,2304]{2,1,0:T(8,128)(2,1)S(1)} copy-done((bf16[4,32,2304]{2,1,0:T(8,128)(2,1)S(1)}, bf16[4,32,2304]{2,1,0:T(8,128)(2,1)}, u32[]{:S(2)}) %copy-start) | copy-done | bytes 589848
  61.4 0.0 copy-start.1
  61.4 1.0 %copy-done.1 = bf16[4,32,1152]{2,1,0:T(8,128)(2,1)S(1)} copy-done((bf16[4,32,1152]{2,1,0:T(8,128)(2,1)S(1)}, bf16[4,32,1152]{2,1,0:T(8,128)(2,1)}, u32[]{:S(2)}) %copy-start.1) | copy-done | bytes 294936
  62.4 6.9 %shard_map.129 = f32[1152,2304]{1,0:T(8,128)} custom-call(bf16[128,1152]{1,0:T(8,128)(2,1)S(1)} %bitcast.11, bf16[128,2304]{1,0:T(8,128)(2,1)S(1)} %bitcast.10), custom_call_target="tpu_custom_call" | custom-call | tf_op jit(solution)/shard_map/pallas_call | solution.py:244
  (3 shorter events, 0.0 us)
Async XLA Ops:
  60.4 1.1 %copy-start = (bf16[4,32,2304]{2,1,0:T(8,128)(2,1)S(1)}, bf16[4,32,2304]{2,1,0:T(8,128)(2,1)}, u32[]{:S(2)}) copy-start(bf16[4,32,2304]{2,1,0:T(8,128)(2,1)} %get-tuple-element.8) | copy-start | bytes 1769476
  61.4 1.0 %copy-start.1 = (bf16[4,32,1152]{2,1,0:T(8,128)(2,1)S(1)}, bf16[4,32,1152]{2,1,0:T(8,128)(2,1)}, u32[]{:S(2)}) copy-start(bf16[4,32,1152]{2,1,0:T(8,128)(2,1)} %get-tuple-element.7) | copy-start | bytes 884740

commit v2 on v1

v2 whole, which is shorter than its diff:
```python
import functools
import math

import jax
import jax.numpy as jnp
import ml_dtypes
import numpy as np
from jax import lax
from jax.experimental import pallas as pl
from jax.experimental.pallas import tpu as pltpu
from jax.sharding import PartitionSpec as P

GRID = 32
CHUNK = 16
LANES = 128
TILE = 256
MAIN = 256
MESH = pl.DeviceIdType.MESH
BF16 = jnp.bfloat16
F32 = jnp.float32


def pad_to(size, unit):
    return -(-size // unit) * unit


def ball(total_g):
    freq = np.arange(-(GRID // 2) + 1, GRID // 2)
    square = freq[:, None, None] ** 2 + freq[None, :, None] ** 2 + freq[None, None, :] ** 2
    return int(np.sort(square.ravel())[total_g])


def split(values):
    high = values.astype(ml_dtypes.bfloat16)
    low = (values - high.astype(np.float64)).astype(ml_dtypes.bfloat16)
    return high, low


def tables(total_g):
    limit = ball(total_g)
    reach = math.isqrt(limit)
    plane = []
    for b in range(0, reach + 1):
        for c in range(-reach, reach + 1):
            if b * b + c * c <= limit and (b > 0 or c >= 0):
                plane.append((b * b + c * c, b, c))
    plane.sort()
    extra = plane[MAIN:]
    short = math.isqrt(limit - extra[0][0]) if extra else -1
    width = pad_to(len(plane), LANES)
    keys = np.full((width,), -1, np.int32)
    bs = np.zeros((width,), np.int64)
    cs = np.zeros((width,), np.int64)
    for at, (_, b, c) in enumerate(plane):
        keys[at] = b * GRID + c + GRID // 2
        bs[at], cs[at] = b, c
    cell = np.arange(GRID * GRID)
    phase = (cell[:, None] // GRID * bs[None] + cell[:, None] % GRID * cs[None]) % GRID
    angle = phase * (2.0 * math.pi / GRID)
    used = keys[None] >= 0
    first = np.concatenate([np.cos(angle) * used, -np.sin(angle) * used], axis=1)
    a = np.arange(-reach, reach + 1)
    angle = (a[:, None] * np.arange(GRID)[None] % GRID) * (2.0 * math.pi / GRID)
    small = np.zeros((len(a), 2, 2, GRID))
    small[:, 0, 0], small[:, 0, 1] = np.cos(angle), np.sin(angle)
    small[:, 1, 0], small[:, 1, 1] = -np.sin(angle), np.cos(angle)
    small = small.reshape(len(a) * 2, 2 * GRID)
    second = np.kron(small, np.eye(CHUNK))
    keys = np.repeat(keys[:, None], TILE, axis=1)
    return reach, short, width, keys, split(first), split(second)


def body(
    reach, short, width, layout,
    tile_info, energy_v, energy_c, g_list, keys, valence_in, conduction_in, *refs,
):
    n_pair, n_grow, n_gcol, per_device, chunks, col_at, row_at = layout
    tables_in, (cols, rows), scratch = refs[:4], refs[4:6], refs[6:]
    valence, conduction, first_h, first_l, second_h, second_l = scratch[:6]
    infos, dens_h, dens_l, next_h, next_l, spec, row_buf = scratch[6:13]
    load_sem, info_send, info_recv, col_send, col_recv, relay_send, relay_recv, row_send, row_recv = scratch[13:]

    me, grow, gcol = lax.axis_index("pair"), lax.axis_index("grow"), lax.axis_index("gcol")
    chip, core = me // 2, me % 2
    n_chip, n_group = n_pair // 2, n_grow * n_gcol
    group = grow * n_gcol + gcol
    sibling = {"pair": chip * 2 + (1 - core)}

    def group_id(step):
        other = (group + step) % n_group
        return {"grow": other // n_gcol, "gcol": other % n_gcol}

    def pair_at(step):
        return (chip + 1 + step // 2) % n_chip * 2 + (core + step % 2) % 2

    own_step = (n_chip - 1) * 2

    loads = [
        pltpu.make_async_copy(source, target, load_sem.at[n])
        for n, (source, target) in enumerate(
            zip((valence_in, conduction_in, *tables_in), scratch[:6])
        )
    ]
    for load in loads:
        load.start()

    barrier = pltpu.get_barrier_semaphore()

    def greet_group(step, carry):
        pl.semaphore_signal(barrier, inc=1, device_id=group_id(step), device_id_type=MESH)
        return carry

    def greet_pair(step, carry):
        @pl.when(step != own_step)
        def _():
            pl.semaphore_signal(
                barrier, inc=1, device_id={"pair": pair_at(step)}, device_id_type=MESH
            )
        return carry

    lax.fori_loop(1, n_group, greet_group, 0)
    lax.fori_loop(0, n_pair, greet_pair, 0)
    pl.semaphore_wait(barrier, n_group - 1 + n_pair - 1)

    def info_copy(step):
        return pltpu.make_async_remote_copy(
            src_ref=tile_info, dst_ref=infos.at[group],
            send_sem=info_send.at[step], recv_sem=info_recv.at[step],
            device_id=group_id(step), device_id_type=MESH,
        )

    def start_info(step, carry):
        info_copy(step).start()
        return carry

    def wait_info(step, carry):
        info_copy(step).wait()
        return carry

    lax.fori_loop(1, n_group, start_info, 0)
    infos[group] = tile_info[...]
    lax.fori_loop(1, n_group, wait_info, 0)

    n_v, n_c = valence.shape[0], conduction.shape[0]
    plane = GRID * GRID
    count = 2 * (2 * reach + 1)
    half = GRID * CHUNK
    together = CHUNK // per_device
    dot = functools.partial(jnp.dot, preferred_element_type=F32)
    loads[0].wait()
    loads[1].wait()

    def transform(n, first_chunk):
        slot = lax.broadcasted_iota(jnp.int32, (CHUNK, LANES), 0)
        info = jnp.zeros((CHUNK, LANES), jnp.int32)
        for d in range(together):
            info = jnp.where(slot // per_device == d, infos[n * together + d], info)
        pick_v = info[:, 0:1] == lax.broadcasted_iota(jnp.int32, (CHUNK, n_v), 1)
        pick_c = info[:, 1:2] == lax.broadcasted_iota(jnp.int32, (CHUNK, n_c), 1)
        live = info[:, 2:3].astype(F32)
        gap = jnp.sum(jnp.where(pick_c, energy_c[...], 0.0), axis=1, keepdims=True) - jnp.sum(
            jnp.where(pick_v, energy_v[...], 0.0), axis=1, keepdims=True
        )
        factor = live * jnp.sqrt(4.0 / gap) / math.sqrt(GRID**3)
        one_v = jnp.where(pick_v, 1.0, 0.0).astype(BF16)
        one_c = jnp.where(pick_c, 1.0, 0.0).astype(BF16)
        for i in range(GRID):
            at = slice(i * plane, (i + 1) * plane)
            dens = dot(one_v, valence[:, at]) * dot(one_c, conduction[:, at])
            high = dens.astype(BF16)
            span = slice(i * CHUNK, (i + 1) * CHUNK)
            dens_h[span, :] = high
            dens_l[span, :] = (dens - high.astype(F32)).astype(BF16)
        if first_chunk:
            loads[2].wait()
            loads[3].wait()
        for part in range(2):
            at = slice(part * width, (part + 1) * width)
            value = (
                dot(dens_h[...], first_h[:, at])
                + dot(dens_l[...], first_h[:, at])
                + dot(dens_h[...], first_l[:, at])
            )
            high = value.astype(BF16)
            next_h[part * half:(part + 1) * half, :] = high
            next_l[part * half:(part + 1) * half, :] = (value - high.astype(F32)).astype(BF16)
        if first_chunk:
            loads[4].wait()
            loads[5].wait()
        value = (
            dot(second_h[...], next_h[...])
            + dot(second_h[...], next_l[...])
            + dot(second_l[...], next_h[...])
        )
        value = value.reshape(count, CHUNK, width) * factor[None]
        spec[n] = value.reshape(count * CHUNK, width).astype(BF16)

    transform(0, True)
    if chunks > 1:
        @pl.loop(1, chunks)
        def _(n):
            transform(n, False)

    height = 2 * CHUNK
    low, high = (reach - short) * height, (reach + short + 1) * height

    def select(n, source, size, out, target):
        cell = g_list[:, pl.ds(pl.multiple_of(source, LANES), size)]
        centre = lambda v: jnp.where(v < GRID // 2, v, v - GRID)
        a = centre(cell // (GRID * GRID))
        b = centre(cell // GRID % GRID)
        c = centre(cell % GRID)
        flip = (b < 0) | ((b == 0) & (c < 0))
        a = jnp.where(flip, -a, a)
        b = jnp.where(flip, -b, b)
        c = jnp.where(flip, -c, c)
        key = b * GRID + c + GRID // 2
        hot = jnp.where(keys[:, :size] == key, 1.0, 0.0).astype(BF16)
        picked = dot(spec[n, :, :MAIN], hot[:MAIN])
        if width > MAIN:
            more = dot(spec[n, low:high, MAIN:], hot[MAIN:])
        total = jnp.zeros((height, size), F32)
        for k in range(2 * reach + 1):
            value = picked[k * height:(k + 1) * height]
            if width > MAIN and low <= k * height < high:
                value = value + more[k * height - low:(k + 1) * height - low]
            total = jnp.where(a == k - reach, value, total)
        imag = total[CHUNK:]
        at = pl.ds(target, size)
        out[n, :CHUNK, at] = total[:CHUNK].astype(BF16)
        out[n, CHUNK:, at] = jnp.where(flip, -imag, imag).astype(BF16)

    def block(source, size, out):
        for n in range(chunks) if chunks == 1 else [None]:
            def run(n):
                @pl.loop(0, size // TILE)
                def _(t):
                    select(n, source + t * TILE, TILE, out, pl.multiple_of(t * TILE, TILE))
                if size % TILE:
                    done = size // TILE * TILE
                    select(n, source + done, size - done, out, done)
            if n is None:
                pl.loop(0, chunks)(run)
            else:
                run(n)

    def col_copy(step):
        peer = (chip + step) % n_chip * 2 + core
        return pltpu.make_async_remote_copy(
            src_ref=cols.at[me], dst_ref=cols.at[me],
            send_sem=col_send.at[step], recv_sem=col_recv.at[step],
            device_id=sibling if step == 0 else {"pair": peer}, device_id_type=MESH,
        )

    def relay_copy(step):
        source = (chip + n_chip - step) % n_chip * 2 + core
        return pltpu.make_async_remote_copy(
            src_ref=cols.at[source], dst_ref=cols.at[source],
            send_sem=relay_send.at[step], recv_sem=relay_recv.at[step],
            device_id=sibling, device_id_type=MESH,
        )

    def row_copy(step):
        return pltpu.make_async_remote_copy(
            src_ref=row_buf.at[step], dst_ref=rows.at[me],
            send_sem=row_send.at[step], recv_sem=row_recv.at[step],
            device_id={"pair": pair_at(step)}, device_id_type=MESH,
        )

    block(col_at(gcol), cols.shape[-1], cols.at[me])
    for step in (*range(1, n_chip), 0):
        col_copy(step).start()

    def row_step(step, carry):
        block(row_at(pair_at(step), grow), rows.shape[-1], row_buf.at[step])

        @pl.when(step != own_step)
        def _():
            row_copy(step).start()
        return carry

    lax.fori_loop(0, own_step, row_step, 0)
    for step in range(1, n_chip):
        col_copy(step).wait_recv()
        relay_copy(step).start()
    lax.fori_loop(own_step, n_pair, row_step, 0)
    rows[me] = row_buf[own_step]

    for step in range(1, n_chip):
        col_copy(step).wait_send()
        relay_copy(step).wait()
    col_copy(0).wait()

    def row_wait(step, carry):
        @pl.when(step != own_step)
        def _():
            row_copy(step).wait()
        return carry

    lax.fori_loop(0, n_pair, row_wait, 0)


def panels(tile_info, energy_v, energy_c, g_list, valence, conduction, total_g, col_pad, row_pad, layout):
    reach, short, width, keys, first, second = tables(total_g)
    n_pair, n_grow, n_gcol, per_device, chunks = layout[:5]
    consts = [jnp.asarray(x) for x in (*first, *second)]
    large = [valence, conduction, *consts]
    args = [tile_info, energy_v, energy_c, g_list, jnp.asarray(keys)]
    height = 2 * CHUNK * (2 * reach + 1)
    half = GRID * CHUNK
    n_group = n_grow * n_gcol
    vmem = pl.BlockSpec(memory_space=pltpu.VMEM)
    dma = pltpu.SemaphoreType.DMA
    return pl.pallas_call(
        functools.partial(body, reach, short, width, layout),
        out_shape=[
            jax.ShapeDtypeStruct((n_pair, chunks, 2 * CHUNK, col_pad), BF16),
            jax.ShapeDtypeStruct((n_pair, chunks, 2 * CHUNK, row_pad), BF16),
        ],
        in_specs=[vmem] * len(args) + [pl.BlockSpec(memory_space=pl.ANY)] * len(large),
        out_specs=[vmem] * 2,
        scratch_shapes=[pltpu.VMEM(x.shape, x.dtype) for x in large] + [
            pltpu.VMEM((n_group, *tile_info.shape), jnp.int32),
            pltpu.VMEM((half, GRID * GRID), BF16),
            pltpu.VMEM((half, GRID * GRID), BF16),
            pltpu.VMEM((2 * half, width), BF16),
            pltpu.VMEM((2 * half, width), BF16),
            pltpu.VMEM((chunks, height, width), BF16),
            pltpu.VMEM((n_pair, chunks, 2 * CHUNK, row_pad), BF16),
            dma((len(large),)),
            dma((n_group,)), dma((n_group,)),
            dma((n_pair // 2,)), dma((n_pair // 2,)),
            dma((n_pair // 2,)), dma((n_pair // 2,)),
            dma((n_pair,)), dma((n_pair,)),
        ],
        compiler_params=pltpu.CompilerParams(
            collective_id=0, has_side_effects=True, vmem_limit_bytes=56 * 2**20
        ),
    )(*args, *large)


def product_kernel(scale, rows, cols, out):
    value = lax.dot_general(
        rows[...], cols[...], (((0,), (0,)), ((), ())), preferred_element_type=F32
    )
    out[...] = value[: out.shape[0], : out.shape[1]] * scale


def product(rows, cols, n_rows, n_cols, scale):
    depth, row_pad = rows.shape
    block = LANES if n_rows % LANES == 0 else n_rows
    return pl.pallas_call(
        functools.partial(product_kernel, scale),
        grid=(n_rows // block,),
        out_shape=jax.ShapeDtypeStruct((n_rows, n_cols), F32),
        in_specs=[
            pl.BlockSpec((depth, pad_to(block, LANES)), lambda n: (0, n)),
            pl.BlockSpec(cols.shape, lambda n: (0, 0)),
        ],
        out_specs=pl.BlockSpec((block, n_cols), lambda n: (n, 0)),
        compiler_params=pltpu.CompilerParams(vmem_limit_bytes=48 * 2**20),
    )(rows, cols)


def local(
    valence,
    conduction,
    valence_energy,
    conduction_energy,
    pair_valence,
    pair_conduction,
    pair_count,
    g_index,
):
    slot_count = pair_valence.shape[0]
    total_g = g_index.shape[0]
    n_pair = lax.axis_size("pair")
    n_grow = lax.axis_size("grow")
    n_gcol = lax.axis_size("gcol")
    sub_rows = total_g // (n_pair * n_grow)
    col_width = total_g // n_gcol
    row_pad, col_pad = pad_to(sub_rows, LANES), pad_to(col_width, LANES)
    live = (jnp.arange(slot_count, dtype=jnp.int32) < pair_count[0]).astype(jnp.int32)
    info = jnp.stack([pair_valence, pair_conduction, live], axis=1)
    info = jnp.pad(jnp.tile(info, (CHUNK // slot_count, 1)), ((0, 0), (0, LANES - 3)))
    if row_pad == sub_rows and col_pad == col_width:
        g_list = g_index[None, :]
        col_at = lambda gcol: gcol * col_width
        row_at = lambda pair, grow: (pair * n_grow + grow) * sub_rows
    else:
        by_col = jnp.pad(g_index.reshape(n_gcol, col_width), ((0, 0), (0, col_pad - col_width)))
        by_row = jnp.pad(g_index.reshape(-1, sub_rows), ((0, 0), (0, row_pad - sub_rows)))
        g_list = jnp.concatenate([by_col.reshape(-1), by_row.reshape(-1)])[None, :]
        col_at = lambda gcol: gcol * col_pad
        row_at = lambda pair, grow: n_gcol * col_pad + (pair * n_grow + grow) * row_pad
    chunks = slot_count * n_grow * n_gcol // CHUNK
    layout = (n_pair, n_grow, n_gcol, slot_count, chunks, col_at, row_at)
    cols, rows = panels(
        info, valence_energy[None, :], conduction_energy[None, :], g_list,
        valence, conduction, total_g, col_pad, row_pad, layout,
    )
    total_slots = slot_count * n_pair * n_grow * n_gcol
    return product(
        rows.reshape(-1, row_pad), cols.reshape(-1, col_pad), sub_rows, col_width,
        -1.0 / math.sqrt(total_slots),
    )


def solution(mesh):
    return jax.shard_map(
        local,
        mesh=mesh,
        in_specs=(
            P(),
            P("pair", None),
            P(),
            P("pair"),
            P(("pair", "grow", "gcol")),
            P(("pair", "grow", "gcol")),
            P(("pair", "grow", "gcol")),
            P(),
        ),
        out_specs=P(("pair", "grow"), "gcol"),
        check_vma=False,
    )
```

time: 70 us -> 42.8 us (0.61)
  blocking collectives: 23.3 us -> 0 us
  Pallas kernels: 40.2 us -> 38.5 us
  local copies, waits for them, and re-layouts: 4.41 us -> 2.72 us
    all_gather x1 -> x0, blocking collectives: 23.3 us -> none  [local(): info = lax.all_gather(info, ('grow', 'gcol'), axis=0, tiled=True)]
    pallas_call x2 -> x1, Pallas kernels: 33.3 us -> 31.7 us  [panels(): pl.pallas_call(functools.partial(body, reach, short, width, layout), out_...]
    dynamic_slice x2 -> x0, local copies, waits for them, and re-layouts: 0.86 us -> none  [the longest x1 0.79 us: local(): lax.dynamic_slice(g_index, (lax.axis_index('gcol') * col_width,), (col_wi...]
    reshape x2 -> x0, local copies, waits for them, and re-layouts: 0.8 us -> none  [the longest x1 0.79 us: local(): g_index.reshape(n_pair, n_grow, sub_rows)]
    unnamed x4 -> x5, local copies, waits for them, and re-layouts: 2.02 us -> 2.11 us
where the time goes in v2:
time: 42.8 us; the launch traced here: 42.6 us
  Pallas kernels  38.5 us (90%)
  local copies, waits for them, and re-layouts  2.72 us (6%)
  other arithmetic  0.69 us (2%)
  between operations  0.68 us (2%)
    pallas_call x1, Pallas kernels, panels(): pl.pallas_call(functools.partial(body, reach, short, width, layout), out_...  31.7 us
    pallas_call x1, Pallas kernels, product(): pl.pallas_call(functools.partial(product_kernel, scale), grid=(n_rows //...  6.88 us
    unnamed x5, local copies, waits for them, and re-layouts  2.11 us

profile of v2, /device:TPU:0, one launch (start us, length us, event | category | flops | bytes accessed | tf_op | source)
XLA Modules:
  0.0 42.6 jit_solution(1194735461780388664)
XLA Ops:
  0.7 0.7 %pad_add_fusion = s32[2,3]{0,1:T(4,128)S(1)} fusion(s32[2,1]{0,1:T(1,128)S(1)} %compare_convert_fusion, s32[2,1]{0,1:T(1,128)} %bitcast.16, s32[2,1]{0,1:T(1,128)} %bitcast.17), kind=kLoop, calls=%fused_computation | loop fusion | flops 12 | bytes 48 | tf_op jit(solution)/shard_map/stack | solution.py:384
  1.3 0.1 copy.17
  1.5 0.6 %pad.4.tile_info = s32[16,128]{1,0:T(8,128)} pad(s32[16,3]{1,0:T(8,128)S(1)} %bitcast.13, s32[]{:T(128)} %constant.5.clone.1), padding=0_0x0_125 | pad | bytes 8388 | tf_op jit(solution)/shard_map/jit(_pad)/pad | solution.py:385
  2.1 31.7 %shard_map.127 = (bf16[4,1,32,2304]{3,2,1,0:T(8,128)(2,1)}, bf16[4,1,32,1152]{3,2,1,0:T(8,128)(2,1)}) custom-call(s32[16,128]{1,0:T(8,128)} %pad.4.tile_info, f32[1,48]{1,0:T(1,128)} %bitcast.14, f32[1,16]{1,0:T(1,128)} %bitcast.15, s32[1,9216]{1,0:T(1,128)} %bitcast.12, s32[384,256]{1,0:T(8,128)} %constant.16.clone.keys, bf16[48,32768]{1,0:T(8,128)(2,1)} %valence_in.1, ...), custom_call_target="tpu_custom_call" | custom-call | tf_op jit(solution)/shard_map/pallas_call | solution.py:314
  33.7 0.0 copy-start
  33.7 1.1 %copy-done = bf16[4,1,32,2304]{3,2,1,0:T(8,128)(2,1)S(1)} copy-done((bf16[4,1,32,2304]{3,2,1,0:T(8,128)(2,1)S(1)}, bf16[4,1,32,2304]{3,2,1,0:T(8,128)(2,1)}, u32[]{:S(2)}) %copy-start) | copy-done | bytes 589848
  34.8 0.0 copy-start.1
  34.8 1.0 %copy-done.1 = bf16[4,1,32,1152]{3,2,1,0:T(8,128)(2,1)S(1)} copy-done((bf16[4,1,32,1152]{3,2,1,0:T(8,128)(2,1)S(1)}, bf16[4,1,32,1152]{3,2,1,0:T(8,128)(2,1)}, u32[]{:S(2)}) %copy-start.1) | copy-done | bytes 294936
  35.7 6.9 %shard_map.128 = f32[1152,2304]{1,0:T(8,128)} custom-call(bf16[128,1152]{1,0:T(8,128)(2,1)S(1)} %bitcast.11, bf16[128,2304]{1,0:T(8,128)(2,1)S(1)} %bitcast.10), custom_call_target="tpu_custom_call" | custom-call | tf_op jit(solution)/shard_map/pallas_call | solution.py:352
  (2 shorter events, 0.0 us)
Async XLA Ops:
  33.7 1.1 %copy-start = (bf16[4,1,32,2304]{3,2,1,0:T(8,128)(2,1)S(1)}, bf16[4,1,32,2304]{3,2,1,0:T(8,128)(2,1)}, u32[]{:S(2)}) copy-start(bf16[4,1,32,2304]{3,2,1,0:T(8,128)(2,1)} %get-tuple-element.8) | copy-start | bytes 1769476
  34.8 1.0 %copy-start.1 = (bf16[4,1,32,1152]{3,2,1,0:T(8,128)(2,1)S(1)}, bf16[4,1,32,1152]{3,2,1,0:T(8,128)(2,1)}, u32[]{:S(2)}) copy-start(bf16[4,1,32,1152]{3,2,1,0:T(8,128)(2,1)} %get-tuple-element.7) | copy-start | bytes 884740

commit v3 on v2

--- a/solution.py
+++ b/solution.py
@@ -59,13 +59,10 @@
     angle = phase * (2.0 * math.pi / GRID)
     used = keys[None] >= 0
     first = np.concatenate([np.cos(angle) * used, -np.sin(angle) * used], axis=1)
-    a = np.arange(-reach, reach + 1)
-    angle = (a[:, None] * np.arange(GRID)[None] % GRID) * (2.0 * math.pi / GRID)
-    small = np.zeros((len(a), 2, 2, GRID))
-    small[:, 0, 0], small[:, 0, 1] = np.cos(angle), np.sin(angle)
-    small[:, 1, 0], small[:, 1, 1] = -np.sin(angle), np.cos(angle)
-    small = small.reshape(len(a) * 2, 2 * GRID)
-    second = np.kron(small, np.eye(CHUNK))
+    points = np.arange(1, GRID // 2 + 1)
+    angle = (np.arange(reach + 1)[:, None] * points[None] % GRID) * (2.0 * math.pi / GRID)
+    second = np.stack([np.cos(angle), np.sin(angle)])
+    second = np.kron(second, np.eye(CHUNK)[None])
     keys = np.repeat(keys[:, None], TILE, axis=1)
     return reach, short, width, keys, split(first), split(second)
 
@@ -76,9 +73,10 @@
 ):
     n_pair, n_grow, n_gcol, per_device, chunks, col_at, row_at = layout
     tables_in, (cols, rows), scratch = refs[:4], refs[4:6], refs[6:]
-    valence, conduction, first_h, first_l, second_h, second_l = scratch[:6]
-    infos, dens_h, dens_l, next_h, next_l, spec, row_buf = scratch[6:13]
-    load_sem, info_send, info_recv, col_send, col_recv, relay_send, relay_recv, row_send, row_recv = scratch[13:]
+    bands, first_h, first_l, second_h, second_l = scratch[:5]
+    infos, dens_h, dens_l, even_h, even_l, odd_h, odd_l, spec, row_buf = scratch[5:14]
+    load_sem, info_send, info_recv, col_send, col_recv, relay_send, relay_recv, row_send, row_recv = scratch[14:]
+    n_v, n_c = valence_in.shape[0], conduction_in.shape[0]
 
     me, grow, gcol = lax.axis_index("pair"), lax.axis_index("grow"), lax.axis_index("gcol")
     chip, core = me // 2, me % 2
@@ -98,7 +96,10 @@
     loads = [
         pltpu.make_async_copy(source, target, load_sem.at[n])
         for n, (source, target) in enumerate(
-            zip((valence_in, conduction_in, *tables_in), scratch[:6])
+            zip(
+                (valence_in, conduction_in, *tables_in),
+                (bands.at[pl.ds(0, n_v)], bands.at[pl.ds(n_v, n_c)], *scratch[1:5]),
+            )
         )
     ]
     for load in loads:
@@ -141,10 +142,7 @@
     infos[group] = tile_info[...]
     lax.fori_loop(1, n_group, wait_info, 0)
 
-    n_v, n_c = valence.shape[0], conduction.shape[0]
     plane = GRID * GRID
-    count = 2 * (2 * reach + 1)
-    half = GRID * CHUNK
     together = CHUNK // per_device
     dot = functools.partial(jnp.dot, preferred_element_type=F32)
     loads[0].wait()
@@ -162,11 +160,15 @@
             jnp.where(pick_v, energy_v[...], 0.0), axis=1, keepdims=True
         )
         factor = live * jnp.sqrt(4.0 / gap) / math.sqrt(GRID**3)
-        one_v = jnp.where(pick_v, 1.0, 0.0).astype(BF16)
-        one_c = jnp.where(pick_c, 1.0, 0.0).astype(BF16)
+        band = lax.broadcasted_iota(jnp.int32, (CHUNK, n_v + n_c), 1)
+        hot = jnp.concatenate(
+            [jnp.where(info[:, 0:1] == band, 1.0, 0.0), jnp.where(info[:, 1:2] + n_v == band, 1.0, 0.0)],
+            axis=0,
+        ).astype(BF16)
         for i in range(GRID):
             at = slice(i * plane, (i + 1) * plane)
-            dens = dot(one_v, valence[:, at]) * dot(one_c, conduction[:, at])
+            both = dot(hot, bands[:, at])
+            dens = both[:CHUNK] * both[CHUNK:]
             high = dens.astype(BF16)
             span = slice(i * CHUNK, (i + 1) * CHUNK)
             dens_h[span, :] = high
@@ -174,26 +176,47 @@
         if first_chunk:
             loads[2].wait()
             loads[3].wait()
+        middle = GRID // 2
+        start = []
         for part in range(2):
             at = slice(part * width, (part + 1) * width)
             value = (
                 dot(dens_h[...], first_h[:, at])
                 + dot(dens_l[...], first_h[:, at])
                 + dot(dens_h[...], first_l[:, at])
-            )
-            high = value.astype(BF16)
-            next_h[part * half:(part + 1) * half, :] = high
-            next_l[part * half:(part + 1) * half, :] = (value - high.astype(F32)).astype(BF16)
+            ).reshape(GRID, CHUNK, width)
+            start.append(value[0])
+            for i in range(1, middle + 1):
+                span = slice((i - 1) * CHUNK, i * CHUNK)
+                even, odd = value[i], jnp.zeros((CHUNK, width), F32)
+                if i < middle:
+                    even, odd = value[i] + value[GRID - i], value[i] - value[GRID - i]
+                for whole, top, rest in ((even, even_h, even_l), (odd, odd_h, odd_l)):
+                    high = whole.astype(BF16)
+                    top[span, at] = high
+                    rest[span, at] = (whole - high.astype(F32)).astype(BF16)
         if first_chunk:
             loads[4].wait()
             loads[5].wait()
-        value = (
-            dot(second_h[...], next_h[...])
-            + dot(second_h[...], next_l[...])
-            + dot(second_l[...], next_h[...])
-        )
-        value = value.reshape(count, CHUNK, width) * factor[None]
-        spec[n] = value.reshape(count * CHUNK, width).astype(BF16)
+        both = []
+        for which, top, rest in ((0, even_h, even_l), (1, odd_h, odd_l)):
+            value = (
+                dot(second_h[which], top[...])
+                + dot(second_h[which], rest[...])
+                + dot(second_l[which], top[...])
+            )
+            both.append(value.reshape(reach + 1, CHUNK, 2 * width))
+        even, odd = both
+        for a in range(reach + 1):
+            even_r, even_i = even[a, :, :width] + start[0], even[a, :, width:] + start[1]
+            odd_r, odd_i = odd[a, :, :width], odd[a, :, width:]
+            parts = [(reach + a, even_r + odd_i, even_i - odd_r)]
+            if a:
+                parts.append((reach - a, even_r - odd_i, even_i + odd_r))
+            for at, real, imag in parts:
+                at = 2 * CHUNK * at
+                spec[n, at:at + CHUNK, :] = (real * factor).astype(BF16)
+                spec[n, at + CHUNK:at + 2 * CHUNK, :] = (imag * factor).astype(BF16)
 
     transform(0, True)
     if chunks > 1:
@@ -309,6 +332,7 @@
     height = 2 * CHUNK * (2 * reach + 1)
     half = GRID * CHUNK
     n_group = n_grow * n_gcol
+    n_v, n_c = valence.shape[0], conduction.shape[0]
     vmem = pl.BlockSpec(memory_space=pltpu.VMEM)
     dma = pltpu.SemaphoreType.DMA
     return pl.pallas_call(
@@ -319,12 +343,12 @@
         ],
         in_specs=[vmem] * len(args) + [pl.BlockSpec(memory_space=pl.ANY)] * len(large),
         out_specs=[vmem] * 2,
-        scratch_shapes=[pltpu.VMEM(x.shape, x.dtype) for x in large] + [
+        scratch_shapes=[pltpu.VMEM((n_v + n_c, GRID**3), BF16)]
+        + [pltpu.VMEM(x.shape, x.dtype) for x in consts] + [
             pltpu.VMEM((n_group, *tile_info.shape), jnp.int32),
             pltpu.VMEM((half, GRID * GRID), BF16),
             pltpu.VMEM((half, GRID * GRID), BF16),
-            pltpu.VMEM((2 * half, width), BF16),
-            pltpu.VMEM((2 * half, width), BF16),
+            *[pltpu.VMEM((half // 2, 2 * width), BF16)] * 4,
             pltpu.VMEM((chunks, height, width), BF16),
             pltpu.VMEM((n_pair, chunks, 2 * CHUNK, row_pad), BF16),
             dma((len(large),)),
@@ -339,26 +363,29 @@
     )(*args, *large)
 
 
-def product_kernel(scale, rows, cols, out):
-    value = lax.dot_general(
-        rows[...], cols[...], (((0,), (0,)), ((), ())), preferred_element_type=F32
-    )
-    out[...] = value[: out.shape[0], : out.shape[1]] * scale
+def product_kernel(scale, rows, cols, out, turned):
+    @pl.when(pl.program_id(0) == 0)
+    def _():
+        turned[...] = rows[...].T
+
+    value = jnp.dot(turned[...], cols[...], preferred_element_type=F32)
+    out[...] = value[: out.shape[0]] * scale
 
 
 def product(rows, cols, n_rows, n_cols, scale):
     depth, row_pad = rows.shape
-    block = LANES if n_rows % LANES == 0 else n_rows
+    block = TILE if n_cols % TILE == 0 else LANES
     return pl.pallas_call(
         functools.partial(product_kernel, scale),
-        grid=(n_rows // block,),
+        grid=(n_cols // block,),
         out_shape=jax.ShapeDtypeStruct((n_rows, n_cols), F32),
         in_specs=[
-            pl.BlockSpec((depth, pad_to(block, LANES)), lambda n: (0, n)),
-            pl.BlockSpec(cols.shape, lambda n: (0, 0)),
+            pl.BlockSpec((depth, row_pad), lambda n: (0, 0)),
+            pl.BlockSpec((depth, block), lambda n: (0, n)),
         ],
-        out_specs=pl.BlockSpec((block, n_cols), lambda n: (n, 0)),
-        compiler_params=pltpu.CompilerParams(vmem_limit_bytes=48 * 2**20),
+        out_specs=pl.BlockSpec((n_rows, block), lambda n: (0, n)),
+        scratch_shapes=[pltpu.VMEM((row_pad, depth), BF16)],
+        compiler_params=pltpu.CompilerParams(vmem_limit_bytes=62 * 2**20),
     )(rows, cols)
 
 

time: 42.8 us -> 40.5 us (0.946)
  local copies, waits for them, and re-layouts: 2.72 us -> 0.71 us
  Pallas kernels: 38.5 us -> 38 us
    unnamed x5 -> x1, local copies, waits for them, and re-layouts: 2.11 us -> 0.09 us
    pallas_call x1, Pallas kernels: 31.7 us -> 29.7 us  [panels(): pl.pallas_call(functools.partial(body, reach, short, width, layout), out_...]
    pallas_call x1, Pallas kernels: 6.88 us -> 8.24 us  [product(): pl.pallas_call(functools.partial(product_kernel, scale), grid=(n_cols //...]
where the time goes in v3:
time: 40.5 us; the launch traced here: 40 us
  Pallas kernels  38 us (94%)
  local copies, waits for them, and re-layouts  0.71 us (2%)
  other arithmetic  0.69 us (2%)
  between operations  0.67 us (2%)
    pallas_call x1, Pallas kernels, panels(): pl.pallas_call(functools.partial(body, reach, short, width, layout), out_...  29.7 us
    pallas_call x1, Pallas kernels, product(): pl.pallas_call(functools.partial(product_kernel, scale), grid=(n_cols //...  8.24 us

profile of v3, /device:TPU:0, one launch (start us, length us, event | category | flops | bytes accessed | tf_op | source)
XLA Modules:
  0.0 40.0 jit_solution(11060460234009319321)
XLA Ops:
  0.7 0.7 %pad_add_fusion = s32[2,3]{0,1:T(4,128)S(1)} fusion(s32[2,1]{0,1:T(1,128)S(1)} %compare_convert_fusion, s32[2,1]{0,1:T(1,128)} %bitcast.16, s32[2,1]{0,1:T(1,128)} %bitcast.17), kind=kLoop, calls=%fused_computation | loop fusion | flops 12 | bytes 48 | tf_op jit(solution)/shard_map/stack | solution.py:411
  1.3 0.1 copy.17
  1.5 0.6 %pad.4.tile_info = s32[16,128]{1,0:T(8,128)} pad(s32[16,3]{1,0:T(8,128)S(1)} %bitcast.13, s32[]{:T(128)} %constant.5.clone.1), padding=0_0x0_125 | pad | bytes 8388 | tf_op jit(solution)/shard_map/jit(_pad)/pad | solution.py:412
  2.1 29.7 %shard_map.127 = (bf16[4,1,32,2304]{3,2,1,0:T(8,128)(2,1)}, bf16[4,1,32,1152]{3,2,1,0:T(8,128)(2,1)}) custom-call(s32[16,128]{1,0:T(8,128)} %pad.4.tile_info, f32[1,48]{1,0:T(1,128)} %bitcast.14, f32[1,16]{1,0:T(1,128)} %bitcast.15, s32[1,9216]{1,0:T(1,128)} %bitcast.12, s32[384,256]{1,0:T(8,128)} %constant.16.clone.keys, bf16[48,32768]{1,0:T(8,128)(2,1)} %valence_in.1, ...), custom_call_target="tpu_custom_call" | custom-call | tf_op jit(solution)/shard_map/pallas_call | solution.py:338
  31.8 8.2 %shard_map.128 = f32[1152,2304]{1,0:T(8,128)} custom-call(bf16[128,1152]{1,0:T(8,128)(2,1)} %bitcast.11, bf16[128,2304]{1,0:T(8,128)(2,1)} %bitcast.10), custom_call_target="tpu_custom_call" | custom-call | tf_op jit(solution)/shard_map/pallas_call | solution.py:378
  (2 shorter events, 0.0 us)

commit v4 on v3

--- a/solution.py
+++ b/solution.py
@@ -11,10 +11,12 @@
 from jax.sharding import PartitionSpec as P
 
 GRID = 32
+BITS = 5
 CHUNK = 16
 LANES = 128
 TILE = 256
 MAIN = 256
+PIECE = 1152
 MESH = pl.DeviceIdType.MESH
 BF16 = jnp.bfloat16
 F32 = jnp.float32
@@ -63,18 +65,19 @@
     angle = (np.arange(reach + 1)[:, None] * points[None] % GRID) * (2.0 * math.pi / GRID)
     second = np.stack([np.cos(angle), np.sin(angle)])
     second = np.kron(second, np.eye(CHUNK)[None])
-    keys = np.repeat(keys[:, None], TILE, axis=1)
+    keys = np.repeat(keys[: pad_to(len(plane), CHUNK), None], TILE, axis=1)
     return reach, short, width, keys, split(first), split(second)
 
 
 def body(
     reach, short, width, layout,
-    tile_info, energy_v, energy_c, g_list, keys, valence_in, conduction_in, *refs,
+    ids_v, ids_c, count, energy_v, energy_c, g_list, keys, valence_in, conduction_in, *refs,
 ):
     n_pair, n_grow, n_gcol, per_device, chunks, col_at, row_at = layout
     tables_in, (cols, rows), scratch = refs[:4], refs[4:6], refs[6:]
     bands, first_h, first_l, second_h, second_l = scratch[:5]
     infos, dens_h, dens_l, even_h, even_l, odd_h, odd_l, spec, row_buf = scratch[5:14]
+    tile_info = infos.at[n_grow * n_gcol]
     load_sem, info_send, info_recv, col_send, col_recv, relay_send, relay_recv, row_send, row_recv = scratch[14:]
     n_v, n_c = valence_in.shape[0], conduction_in.shape[0]
 
@@ -105,6 +108,15 @@
     for load in loads:
         load.start()
 
+    slot = lax.broadcasted_iota(jnp.int32, (CHUNK, LANES), 0) % per_device
+    lane = lax.broadcasted_iota(jnp.int32, (CHUNK, LANES), 1)
+    mine = jnp.zeros((CHUNK, LANES), jnp.int32)
+    for j in range(per_device):
+        live = jnp.where(count[0] > j, 1, 0)
+        row = jnp.where(lane == 0, ids_v[j], jnp.where(lane == 1, ids_c[j], live))
+        mine = jnp.where(slot == j, row, mine)
+    tile_info[...] = mine
+
     barrier = pltpu.get_barrier_semaphore()
 
     def greet_group(step, carry):
@@ -139,7 +151,7 @@
         return carry
 
     lax.fori_loop(1, n_group, start_info, 0)
-    infos[group] = tile_info[...]
+    infos[group] = mine
     lax.fori_loop(1, n_group, wait_info, 0)
 
     plane = GRID * GRID
@@ -230,9 +242,9 @@
     def select(n, source, size, out, target):
         cell = g_list[:, pl.ds(pl.multiple_of(source, LANES), size)]
         centre = lambda v: jnp.where(v < GRID // 2, v, v - GRID)
-        a = centre(cell // (GRID * GRID))
-        b = centre(cell // GRID % GRID)
-        c = centre(cell % GRID)
+        a = centre(cell >> (2 * BITS))
+        b = centre((cell >> BITS) & (GRID - 1))
+        c = centre(cell & (GRID - 1))
         flip = (b < 0) | ((b == 0) & (c < 0))
         a = jnp.where(flip, -a, a)
         b = jnp.where(flip, -b, b)
@@ -241,7 +253,7 @@
         hot = jnp.where(keys[:, :size] == key, 1.0, 0.0).astype(BF16)
         picked = dot(spec[n, :, :MAIN], hot[:MAIN])
         if width > MAIN:
-            more = dot(spec[n, low:high, MAIN:], hot[MAIN:])
+            more = dot(spec[n, low:high, MAIN:keys.shape[0]], hot[MAIN:])
         total = jnp.zeros((height, size), F32)
         for k in range(2 * reach + 1):
             value = picked[k * height:(k + 1) * height]
@@ -254,18 +266,24 @@
         out[n, CHUNK:, at] = jnp.where(flip, -imag, imag).astype(BF16)
 
     def block(source, size, out):
-        for n in range(chunks) if chunks == 1 else [None]:
-            def run(n):
-                @pl.loop(0, size // TILE)
-                def _(t):
-                    select(n, source + t * TILE, TILE, out, pl.multiple_of(t * TILE, TILE))
-                if size % TILE:
-                    done = size // TILE * TILE
-                    select(n, source + done, size - done, out, done)
-            if n is None:
-                pl.loop(0, chunks)(run)
+        piece = max(x for x in range(LANES, PIECE + 1, LANES) if size % x == 0)
+
+        def run(n):
+            def part(t):
+                for done in range(0, piece, TILE):
+                    at = t * piece + done
+                    at = at if isinstance(at, int) else pl.multiple_of(at, LANES)
+                    select(n, source + at, min(TILE, piece - done), out, at)
+
+            if size == piece:
+                part(0)
             else:
-                run(n)
+                pl.loop(0, size // piece)(part)
+
+        if chunks == 1:
+            run(0)
+        else:
+            pl.loop(0, chunks)(run)
 
     def col_copy(step):
         peer = (chip + step) % n_chip * 2 + core
@@ -323,12 +341,12 @@
     lax.fori_loop(0, n_pair, row_wait, 0)
 
 
-def panels(tile_info, energy_v, energy_c, g_list, valence, conduction, total_g, col_pad, row_pad, layout):
+def panels(ids, energy_v, energy_c, g_list, valence, conduction, total_g, col_pad, row_pad, layout):
     reach, short, width, keys, first, second = tables(total_g)
     n_pair, n_grow, n_gcol, per_device, chunks = layout[:5]
     consts = [jnp.asarray(x) for x in (*first, *second)]
     large = [valence, conduction, *consts]
-    args = [tile_info, energy_v, energy_c, g_list, jnp.asarray(keys)]
+    args = [energy_v, energy_c, g_list, jnp.asarray(keys)]
     height = 2 * CHUNK * (2 * reach + 1)
     half = GRID * CHUNK
     n_group = n_grow * n_gcol
@@ -341,11 +359,12 @@
             jax.ShapeDtypeStruct((n_pair, chunks, 2 * CHUNK, col_pad), BF16),
             jax.ShapeDtypeStruct((n_pair, chunks, 2 * CHUNK, row_pad), BF16),
         ],
-        in_specs=[vmem] * len(args) + [pl.BlockSpec(memory_space=pl.ANY)] * len(large),
+        in_specs=[pl.BlockSpec(memory_space=pltpu.SMEM)] * len(ids) + [vmem] * len(args)
+        + [pl.BlockSpec(memory_space=pl.ANY)] * len(large),
         out_specs=[vmem] * 2,
         scratch_shapes=[pltpu.VMEM((n_v + n_c, GRID**3), BF16)]
         + [pltpu.VMEM(x.shape, x.dtype) for x in consts] + [
-            pltpu.VMEM((n_group, *tile_info.shape), jnp.int32),
+            pltpu.VMEM((n_group + 1, CHUNK, LANES), jnp.int32),
             pltpu.VMEM((half, GRID * GRID), BF16),
             pltpu.VMEM((half, GRID * GRID), BF16),
             *[pltpu.VMEM((half // 2, 2 * width), BF16)] * 4,
@@ -360,31 +379,35 @@
         compiler_params=pltpu.CompilerParams(
             collective_id=0, has_side_effects=True, vmem_limit_bytes=56 * 2**20
         ),
-    )(*args, *large)
-
-
-def product_kernel(scale, rows, cols, out, turned):
-    @pl.when(pl.program_id(0) == 0)
-    def _():
-        turned[...] = rows[...].T
-
-    value = jnp.dot(turned[...], cols[...], preferred_element_type=F32)
-    out[...] = value[: out.shape[0]] * scale
+    )(*ids, *args, *large)
+
+
+def product_kernel(scale, pieces, rows, cols, out, turned, held, sem):
+    turned[...] = rows[...].T
+    step = out.shape[0] // pieces
+    copies = []
+    for n in range(pieces):
+        at = pl.ds(n * step, step)
+        held[at, :] = jnp.dot(turned[at, :], cols[...], preferred_element_type=F32) * scale
+        copies.append(pltpu.make_async_copy(held.at[at], out.at[at], sem.at[n]))
+        copies[-1].start()
+    for copy in copies:
+        copy.wait()
 
 
 def product(rows, cols, n_rows, n_cols, scale):
     depth, row_pad = rows.shape
-    block = TILE if n_cols % TILE == 0 else LANES
+    pieces = max(x for x in range(1, 9) if n_rows % (16 * x) == 0)
     return pl.pallas_call(
-        functools.partial(product_kernel, scale),
-        grid=(n_cols // block,),
+        functools.partial(product_kernel, scale, pieces),
         out_shape=jax.ShapeDtypeStruct((n_rows, n_cols), F32),
-        in_specs=[
-            pl.BlockSpec((depth, row_pad), lambda n: (0, 0)),
-            pl.BlockSpec((depth, block), lambda n: (0, n)),
+        in_specs=[pl.BlockSpec(memory_space=pltpu.VMEM)] * 2,
+        out_specs=pl.BlockSpec(memory_space=pl.ANY),
+        scratch_shapes=[
+            pltpu.VMEM((row_pad, depth), BF16),
+            pltpu.VMEM((n_rows, n_cols), F32),
+            pltpu.SemaphoreType.DMA((pieces,)),
         ],
-        out_specs=pl.BlockSpec((n_rows, block), lambda n: (0, n)),
-        scratch_shapes=[pltpu.VMEM((row_pad, depth), BF16)],
         compiler_params=pltpu.CompilerParams(vmem_limit_bytes=62 * 2**20),
     )(rows, cols)
 
@@ -407,9 +430,6 @@
     sub_rows = total_g // (n_pair * n_grow)
     col_width = total_g // n_gcol
     row_pad, col_pad = pad_to(sub_rows, LANES), pad_to(col_width, LANES)
-    live = (jnp.arange(slot_count, dtype=jnp.int32) < pair_count[0]).astype(jnp.int32)
-    info = jnp.stack([pair_valence, pair_conduction, live], axis=1)
-    info = jnp.pad(jnp.tile(info, (CHUNK // slot_count, 1)), ((0, 0), (0, LANES - 3)))
     if row_pad == sub_rows and col_pad == col_width:
         g_list = g_index[None, :]
         col_at = lambda gcol: gcol * col_width
@@ -423,7 +443,7 @@
     chunks = slot_count * n_grow * n_gcol // CHUNK
     layout = (n_pair, n_grow, n_gcol, slot_count, chunks, col_at, row_at)
     cols, rows = panels(
-        info, valence_energy[None, :], conduction_energy[None, :], g_list,
+        (pair_valence, pair_conduction, pair_count), valence_energy[None, :], conduction_energy[None, :], g_list,
         valence, conduction, total_g, col_pad, row_pad, layout,
     )
     total_slots = slot_count * n_pair * n_grow * n_gcol

time: 40.5 us -> 33.5 us (0.83)
  Pallas kernels: 38 us -> 32.6 us
  local copies, waits for them, and re-layouts: 0.71 us -> 0 us
  other arithmetic: 0.69 us -> 0 us
    pallas_call x1, Pallas kernels: 29.7 us -> 27 us  [panels(): pl.pallas_call(functools.partial(body, reach, short, width, layout), out_...]
    pallas_call x1, Pallas kernels: 8.24 us -> 5.62 us  [product(): pl.pallas_call(functools.partial(product_kernel, scale, pieces), out_shap...]
    another operation x1 -> x0, other arithmetic: 0.68 us -> none  [local(): info = jnp.stack([pair_valence, pair_conduction, live], axis=1)]
    pad x1 -> x0, local copies, waits for them, and re-layouts: 0.6 us -> none  [local(): jnp.pad(jnp.tile(info, (CHUNK // slot_count, 1)), ((0, 0), (0, LANES - 3)))]
where the time goes in v4:
time: 33.5 us; the launch traced here: 33.3 us
  Pallas kernels  32.6 us (97%)
  between operations  0.66 us (2%)
    pallas_call x1, Pallas kernels, panels(): pl.pallas_call(functools.partial(body, reach, short, width, layout), out_...  27 us
    pallas_call x1, Pallas kernels, product(): pl.pallas_call(functools.partial(product_kernel, scale, pieces), out_shap...  5.62 us

profile of v4, /device:TPU:0, one launch (start us, length us, event | category | flops | bytes accessed | tf_op | source)
XLA Modules:
  0.0 33.3 jit_solution(11231215024400372918)
XLA Ops:
  0.7 27.0 %shard_map.127 = (bf16[4,1,32,2304]{3,2,1,0:T(8,128)(2,1)}, bf16[4,1,32,1152]{3,2,1,0:T(8,128)(2,1)}) custom-call(s32[2]{0:T(128)} %ids_v.1, s32[2]{0:T(128)} %ids_c.1, s32[1]{0:T(128)S(6)} %copy.14.count, f32[1,48]{1,0:T(1,128)} %bitcast.8, f32[1,16]{1,0:T(1,128)} %bitcast.9, s32[1,9216]{1,0:T(1,128)} %bitcast.7, s32[288,256]{1,0:T(8,128)} %constant.14.clone.keys, ...), custom_call_target="tpu_custom_call" | custom-call | tf_op jit(solution)/shard_map/pallas_call | solution.py:356
  27.7 5.6 %shard_map.128 = f32[1152,2304]{1,0:T(8,128)} custom-call(bf16[128,1152]{1,0:T(8,128)(2,1)} %bitcast.6, bf16[128,2304]{1,0:T(8,128)(2,1)} %bitcast.5), custom_call_target="tpu_custom_call" | custom-call | tf_op jit(solution)/shard_map/pallas_call | solution.py:401

commit v5 on v4

--- a/solution.py
+++ b/solution.py
@@ -14,6 +14,7 @@
 BITS = 5
 CHUNK = 16
 LANES = 128
+SUBLANES = 8
 TILE = 256
 MAIN = 256
 PIECE = 1152
@@ -76,9 +77,9 @@
     n_pair, n_grow, n_gcol, per_device, chunks, col_at, row_at = layout
     tables_in, (cols, rows), scratch = refs[:4], refs[4:6], refs[6:]
     bands, first_h, first_l, second_h, second_l = scratch[:5]
-    infos, dens_h, dens_l, even_h, even_l, odd_h, odd_l, spec, row_buf = scratch[5:14]
+    infos, dens_h, dens_l, even_h, even_l, odd_h, odd_l, spec, row_buf, hots, facts = scratch[5:16]
     tile_info = infos.at[n_grow * n_gcol]
-    load_sem, info_send, info_recv, col_send, col_recv, relay_send, relay_recv, row_send, row_recv = scratch[14:]
+    load_sem, info_send, info_recv, col_send, col_recv, relay_send, relay_recv, row_send, row_recv = scratch[16:]
     n_v, n_c = valence_in.shape[0], conduction_in.shape[0]
 
     me, grow, gcol = lax.axis_index("pair"), lax.axis_index("grow"), lax.axis_index("gcol")
@@ -117,6 +118,34 @@
         mine = jnp.where(slot == j, row, mine)
     tile_info[...] = mine
 
+    def prepare(source, target, size):
+        cell = g_list[:, pl.ds(source, size)]
+        cell = jnp.broadcast_to(cell, (SUBLANES, size))
+        centre = lambda v: jnp.where(v < GRID // 2, v, v - GRID)
+        a = centre(cell >> (2 * BITS))
+        b = centre((cell >> BITS) & (GRID - 1))
+        c = centre(cell & (GRID - 1))
+        flip = (b < 0) | ((b == 0) & (c < 0))
+        a = jnp.where(flip, -a, a)
+        b = jnp.where(flip, -b, b)
+        c = jnp.where(flip, -c, c)
+        key = b * GRID + c + GRID // 2
+        here = pl.ds(target, size)
+        facts[0, :, here] = a.astype(F32)
+        facts[1, :, here] = jnp.where(flip, -1.0, 1.0)
+        for at in range(0, keys.shape[0], CHUNK):
+            match = keys[at:at + CHUNK, :size] == jnp.concatenate([key] * (CHUNK // SUBLANES), axis=0)
+            hots[at:at + CHUNK, here] = jnp.where(match, 1.0, 0.0).astype(BF16)
+
+    def prepare_block(source, target, size):
+        @pl.loop(0, size // LANES)
+        def _(t):
+            prepare(
+                pl.multiple_of(source + t * LANES, LANES),
+                pl.multiple_of(target + t * LANES, LANES), LANES,
+            )
+
+    col_pad, row_pad = cols.shape[-1], rows.shape[-1]
     barrier = pltpu.get_barrier_semaphore()
 
     def greet_group(step, carry):
@@ -133,6 +162,7 @@
 
     lax.fori_loop(1, n_group, greet_group, 0)
     lax.fori_loop(0, n_pair, greet_pair, 0)
+    prepare_block(col_at(gcol), 0, col_pad)
     pl.semaphore_wait(barrier, n_group - 1 + n_pair - 1)
 
     def info_copy(step):
@@ -152,6 +182,11 @@
 
     lax.fori_loop(1, n_group, start_info, 0)
     infos[group] = mine
+
+    @pl.loop(0, n_pair)
+    def _(step):
+        prepare_block(row_at(pair_at(step), grow), col_pad + step * row_pad, row_pad)
+
     lax.fori_loop(1, n_group, wait_info, 0)
 
     plane = GRID * GRID
@@ -240,64 +275,55 @@
     low, high = (reach - short) * height, (reach + short + 1) * height
 
     def select(n, source, size, out, target):
-        cell = g_list[:, pl.ds(pl.multiple_of(source, LANES), size)]
-        centre = lambda v: jnp.where(v < GRID // 2, v, v - GRID)
-        a = centre(cell >> (2 * BITS))
-        b = centre((cell >> BITS) & (GRID - 1))
-        c = centre(cell & (GRID - 1))
-        flip = (b < 0) | ((b == 0) & (c < 0))
-        a = jnp.where(flip, -a, a)
-        b = jnp.where(flip, -b, b)
-        c = jnp.where(flip, -c, c)
-        key = b * GRID + c + GRID // 2
-        hot = jnp.where(keys[:, :size] == key, 1.0, 0.0).astype(BF16)
-        picked = dot(spec[n, :, :MAIN], hot[:MAIN])
+        here = pl.ds(source, size)
+        a, sign = facts[0, :, here], facts[1, :, here]
+        a = jnp.concatenate([a] * (2 * CHUNK // SUBLANES), axis=0)
+        sign = jnp.concatenate([sign] * (CHUNK // SUBLANES), axis=0)
+        hot = hots.at[:, here]
+        picked = dot(spec[n, :, :MAIN], hot[:MAIN, :])
         if width > MAIN:
-            more = dot(spec[n, low:high, MAIN:keys.shape[0]], hot[MAIN:])
+            more = dot(spec[n, low:high, MAIN:keys.shape[0]], hot[MAIN:, :])
         total = jnp.zeros((height, size), F32)
         for k in range(2 * reach + 1):
             value = picked[k * height:(k + 1) * height]
             if width > MAIN and low <= k * height < high:
                 value = value + more[k * height - low:(k + 1) * height - low]
-            total = jnp.where(a == k - reach, value, total)
+            total = jnp.where(a == float(k - reach), value, total)
         imag = total[CHUNK:]
         at = pl.ds(target, size)
         out[n, :CHUNK, at] = total[:CHUNK].astype(BF16)
-        out[n, CHUNK:, at] = jnp.where(flip, -imag, imag).astype(BF16)
-
-    def block(source, size, out):
-        piece = max(x for x in range(LANES, PIECE + 1, LANES) if size % x == 0)
-
+        out[n, CHUNK:, at] = (imag * sign).astype(BF16)
+
+    def block(source, target, size, out):
         def run(n):
-            def part(t):
-                for done in range(0, piece, TILE):
-                    at = t * piece + done
-                    at = at if isinstance(at, int) else pl.multiple_of(at, LANES)
-                    select(n, source + at, min(TILE, piece - done), out, at)
-
-            if size == piece:
-                part(0)
-            else:
-                pl.loop(0, size // piece)(part)
+            for done in range(0, size, TILE):
+                at = source + done
+                at = at if isinstance(at, int) else pl.multiple_of(at, LANES)
+                select(n, at, min(TILE, size - done), out, target + done)
 
         if chunks == 1:
             run(0)
         else:
             pl.loop(0, chunks)(run)
 
-    def col_copy(step):
+    piece = max(x for x in range(LANES, PIECE + 1, LANES) if col_pad % x == 0)
+    parts = col_pad // piece
+
+    def col_copy(step, part):
         peer = (chip + step) % n_chip * 2 + core
+        here = cols.at[me, :, :, pl.ds(part * piece, piece)]
         return pltpu.make_async_remote_copy(
-            src_ref=cols.at[me], dst_ref=cols.at[me],
-            send_sem=col_send.at[step], recv_sem=col_recv.at[step],
+            src_ref=here, dst_ref=here,
+            send_sem=col_send.at[step, part], recv_sem=col_recv.at[step, part],
             device_id=sibling if step == 0 else {"pair": peer}, device_id_type=MESH,
         )
 
-    def relay_copy(step):
+    def relay_copy(step, part):
         source = (chip + n_chip - step) % n_chip * 2 + core
+        here = cols.at[source, :, :, pl.ds(part * piece, piece)]
         return pltpu.make_async_remote_copy(
-            src_ref=cols.at[source], dst_ref=cols.at[source],
-            send_sem=relay_send.at[step], recv_sem=relay_recv.at[step],
+            src_ref=here, dst_ref=here,
+            send_sem=relay_send.at[step, part], recv_sem=relay_recv.at[step, part],
             device_id=sibling, device_id_type=MESH,
         )
 
@@ -308,12 +334,13 @@
             device_id={"pair": pair_at(step)}, device_id_type=MESH,
         )
 
-    block(col_at(gcol), cols.shape[-1], cols.at[me])
-    for step in (*range(1, n_chip), 0):
-        col_copy(step).start()
+    for part in range(parts):
+        block(part * piece, part * piece, piece, cols.at[me])
+        for step in (*range(1, n_chip), 0):
+            col_copy(step, part).start()
 
     def row_step(step, carry):
-        block(row_at(pair_at(step), grow), rows.shape[-1], row_buf.at[step])
+        block(col_pad + step * row_pad, 0, row_pad, row_buf.at[step])
 
         @pl.when(step != own_step)
         def _():
@@ -321,16 +348,18 @@
         return carry
 
     lax.fori_loop(0, own_step, row_step, 0)
-    for step in range(1, n_chip):
-        col_copy(step).wait_recv()
-        relay_copy(step).start()
+    for part in range(parts):
+        for step in range(1, n_chip):
+            col_copy(step, part).wait_recv()
+            relay_copy(step, part).start()
     lax.fori_loop(own_step, n_pair, row_step, 0)
     rows[me] = row_buf[own_step]
 
-    for step in range(1, n_chip):
-        col_copy(step).wait_send()
-        relay_copy(step).wait()
-    col_copy(0).wait()
+    for part in range(parts):
+        for step in range(1, n_chip):
+            col_copy(step, part).wait_send()
+            relay_copy(step, part).wait()
+        col_copy(0, part).wait()
 
     def row_wait(step, carry):
         @pl.when(step != own_step)
@@ -370,10 +399,11 @@
             *[pltpu.VMEM((half // 2, 2 * width), BF16)] * 4,
             pltpu.VMEM((chunks, height, width), BF16),
             pltpu.VMEM((n_pair, chunks, 2 * CHUNK, row_pad), BF16),
+            pltpu.VMEM((keys.shape[0], col_pad + n_pair * row_pad), BF16),
+            pltpu.VMEM((2, SUBLANES, col_pad + n_pair * row_pad), F32),
             dma((len(large),)),
             dma((n_group,)), dma((n_group,)),
-            dma((n_pair // 2,)), dma((n_pair // 2,)),
-            dma((n_pair // 2,)), dma((n_pair // 2,)),
+            *[dma((n_pair // 2, col_pad // LANES))] * 4,
             dma((n_pair,)), dma((n_pair,)),
         ],
         compiler_params=pltpu.CompilerParams(

time: 33.5 us -> 33.8 us (level)
  no operation moved by 1% of the time
where the time goes in v5:
time: 33.8 us; the launch traced here: 33.6 us
  Pallas kernels  32.9 us (97%)
  between operations  0.66 us (2%)
    pallas_call x1, Pallas kernels, panels(): pl.pallas_call(functools.partial(body, reach, short, width, layout), out_...  27.3 us
    pallas_call x1, Pallas kernels, product(): pl.pallas_call(functools.partial(product_kernel, scale, pieces), out_shap...  5.62 us

profile of v5, /device:TPU:0, one launch (start us, length us, event | category | flops | bytes accessed | tf_op | source)
XLA Modules:
  0.0 33.6 jit_solution(8529930461300822460)
XLA Ops:
  0.7 27.3 %shard_map.127 = (bf16[4,1,32,2304]{3,2,1,0:T(8,128)(2,1)}, bf16[4,1,32,1152]{3,2,1,0:T(8,128)(2,1)}) custom-call(s32[2]{0:T(128)} %ids_v.1, s32[2]{0:T(128)} %ids_c.1, s32[1]{0:T(128)S(6)} %copy.14.count, f32[1,48]{1,0:T(1,128)} %bitcast.8, f32[1,16]{1,0:T(1,128)} %bitcast.9, s32[1,9216]{1,0:T(1,128)} %bitcast.7, s32[288,256]{1,0:T(8,128)} %constant.14.clone.keys, ...), custom_call_target="tpu_custom_call" | custom-call | tf_op jit(solution)/shard_map/pallas_call | solution.py:385
  28.0 5.6 %shard_map.128 = f32[1152,2304]{1,0:T(8,128)} custom-call(bf16[128,1152]{1,0:T(8,128)(2,1)} %bitcast.6, bf16[128,2304]{1,0:T(8,128)(2,1)} %bitcast.5), custom_call_target="tpu_custom_call" | custom-call | tf_op jit(solution)/shard_map/pallas_call | solution.py:431

commit v6 on v5

--- a/solution.py
+++ b/solution.py
@@ -118,7 +118,7 @@
         mine = jnp.where(slot == j, row, mine)
     tile_info[...] = mine
 
-    def prepare(source, target, size):
+    def facts_of(source, size):
         cell = g_list[:, pl.ds(source, size)]
         cell = jnp.broadcast_to(cell, (SUBLANES, size))
         centre = lambda v: jnp.where(v < GRID // 2, v, v - GRID)
@@ -130,12 +130,18 @@
         b = jnp.where(flip, -b, b)
         c = jnp.where(flip, -c, c)
         key = b * GRID + c + GRID // 2
+        key = jnp.concatenate([key] * (CHUNK // SUBLANES), axis=0)
+        hot = [
+            jnp.where(keys[at:at + CHUNK, :size] == key, 1.0, 0.0).astype(BF16)
+            for at in range(0, keys.shape[0], CHUNK)
+        ]
+        return a.astype(F32), jnp.where(flip, -1.0, 1.0), hot
+
+    def prepare(source, target, size):
         here = pl.ds(target, size)
-        facts[0, :, here] = a.astype(F32)
-        facts[1, :, here] = jnp.where(flip, -1.0, 1.0)
-        for at in range(0, keys.shape[0], CHUNK):
-            match = keys[at:at + CHUNK, :size] == jnp.concatenate([key] * (CHUNK // SUBLANES), axis=0)
-            hots[at:at + CHUNK, here] = jnp.where(match, 1.0, 0.0).astype(BF16)
+        facts[0, :, here], facts[1, :, here], hot = facts_of(source, size)
+        for n, rows_of in enumerate(hot):
+            hots[n * CHUNK:(n + 1) * CHUNK, here] = rows_of
 
     def prepare_block(source, target, size):
         @pl.loop(0, size // LANES)
@@ -183,9 +189,7 @@
     lax.fori_loop(1, n_group, start_info, 0)
     infos[group] = mine
 
-    @pl.loop(0, n_pair)
-    def _(step):
-        prepare_block(row_at(pair_at(step), grow), col_pad + step * row_pad, row_pad)
+    prepare_block(row_at(pair_at(0), grow), col_pad, row_pad)
 
     lax.fori_loop(1, n_group, wait_info, 0)
 
@@ -274,15 +278,22 @@
     height = 2 * CHUNK
     low, high = (reach - short) * height, (reach + short + 1) * height
 
-    def select(n, source, size, out, target):
+    def select(n, source, size, out, target, ready):
         here = pl.ds(source, size)
-        a, sign = facts[0, :, here], facts[1, :, here]
+        if ready:
+            a, sign = facts[0, :, here], facts[1, :, here]
+            hot = [hots[:MAIN, here], hots[MAIN:, here]]
+        else:
+            a, sign, hot = facts_of(source, size)
+            cut = MAIN // CHUNK
+            hot = [jnp.concatenate(hot[:cut], axis=0)] + [
+                jnp.concatenate(hot[cut:], axis=0) for _ in range(1) if width > MAIN
+            ]
         a = jnp.concatenate([a] * (2 * CHUNK // SUBLANES), axis=0)
         sign = jnp.concatenate([sign] * (CHUNK // SUBLANES), axis=0)
-        hot = hots.at[:, here]
-        picked = dot(spec[n, :, :MAIN], hot[:MAIN, :])
+        picked = dot(spec[n, :, :MAIN], hot[0])
         if width > MAIN:
-            more = dot(spec[n, low:high, MAIN:keys.shape[0]], hot[MAIN:, :])
+            more = dot(spec[n, low:high, MAIN:keys.shape[0]], hot[1])
         total = jnp.zeros((height, size), F32)
         for k in range(2 * reach + 1):
             value = picked[k * height:(k + 1) * height]
@@ -294,12 +305,12 @@
         out[n, :CHUNK, at] = total[:CHUNK].astype(BF16)
         out[n, CHUNK:, at] = (imag * sign).astype(BF16)
 
-    def block(source, target, size, out):
+    def block(source, size, out, target, ready):
         def run(n):
             for done in range(0, size, TILE):
                 at = source + done
                 at = at if isinstance(at, int) else pl.multiple_of(at, LANES)
-                select(n, at, min(TILE, size - done), out, target + done)
+                select(n, at, min(TILE, size - done), out, target + done, ready)
 
         if chunks == 1:
             run(0)
@@ -335,19 +346,22 @@
         )
 
     for part in range(parts):
-        block(part * piece, part * piece, piece, cols.at[me])
+        block(part * piece, piece, cols.at[me], part * piece, True)
         for step in (*range(1, n_chip), 0):
             col_copy(step, part).start()
 
     def row_step(step, carry):
-        block(col_pad + step * row_pad, 0, row_pad, row_buf.at[step])
+        first = isinstance(step, int)
+        source = col_pad if first else row_at(pair_at(step), grow)
+        block(source, row_pad, row_buf.at[step], 0, first)
 
         @pl.when(step != own_step)
         def _():
             row_copy(step).start()
         return carry
 
-    lax.fori_loop(0, own_step, row_step, 0)
+    row_step(0, 0)
+    lax.fori_loop(1, own_step, row_step, 0)
     for part in range(parts):
         for step in range(1, n_chip):
             col_copy(step, part).wait_recv()
@@ -399,8 +413,8 @@
             *[pltpu.VMEM((half // 2, 2 * width), BF16)] * 4,
             pltpu.VMEM((chunks, height, width), BF16),
             pltpu.VMEM((n_pair, chunks, 2 * CHUNK, row_pad), BF16),
-            pltpu.VMEM((keys.shape[0], col_pad + n_pair * row_pad), BF16),
-            pltpu.VMEM((2, SUBLANES, col_pad + n_pair * row_pad), F32),
+            pltpu.VMEM((keys.shape[0], col_pad + row_pad), BF16),
+            pltpu.VMEM((2, SUBLANES, col_pad + row_pad), F32),
             dma((len(large),)),
             dma((n_group,)), dma((n_group,)),
             *[dma((n_pair // 2, col_pad // LANES))] * 4,
@@ -414,10 +428,9 @@
 
 def product_kernel(scale, pieces, rows, cols, out, turned, held, sem):
     turned[...] = rows[...].T
-    step = out.shape[0] // pieces
     copies = []
-    for n in range(pieces):
-        at = pl.ds(n * step, step)
+    for n, (start, step) in enumerate(pieces):
+        at = pl.ds(start, step)
         held[at, :] = jnp.dot(turned[at, :], cols[...], preferred_element_type=F32) * scale
         copies.append(pltpu.make_async_copy(held.at[at], out.at[at], sem.at[n]))
         copies[-1].start()
@@ -427,7 +440,11 @@
 
 def product(rows, cols, n_rows, n_cols, scale):
     depth, row_pad = rows.shape
-    pieces = max(x for x in range(1, 9) if n_rows % (16 * x) == 0)
+    pieces, start = [], 0
+    while start < n_rows:
+        step = min(CHUNK * (1 << min(len(pieces) + 1, 3)), n_rows - start)
+        pieces.append((start, step))
+        start += step
     return pl.pallas_call(
         functools.partial(product_kernel, scale, pieces),
         out_shape=jax.ShapeDtypeStruct((n_rows, n_cols), F32),
@@ -436,7 +453,7 @@
         scratch_shapes=[
             pltpu.VMEM((row_pad, depth), BF16),
             pltpu.VMEM((n_rows, n_cols), F32),
-            pltpu.SemaphoreType.DMA((pieces,)),
+            pltpu.SemaphoreType.DMA((len(pieces),)),
         ],
         compiler_params=pltpu.CompilerParams(vmem_limit_bytes=62 * 2**20),
     )(rows, cols)

time: 33.8 us -> 33.5 us (level)
  no operation moved by 1% of the time
where the time goes in v6:
time: 33.5 us; the launch traced here: 33.4 us
  Pallas kernels  32.7 us (98%)
  between operations  0.66 us (2%)
    pallas_call x1, Pallas kernels, panels(): pl.pallas_call(functools.partial(body, reach, short, width, layout), out_...  27.3 us
    pallas_call x1, Pallas kernels, product(): pl.pallas_call(functools.partial(product_kernel, scale, pieces), out_shap...  5.46 us

profile of v6, /device:TPU:0, one launch (start us, length us, event | category | flops | bytes accessed | tf_op | source)
XLA Modules:
  0.0 33.4 jit_solution(8403108217760808046)
XLA Ops:
  0.7 27.3 %shard_map.127 = (bf16[4,1,32,2304]{3,2,1,0:T(8,128)(2,1)}, bf16[4,1,32,1152]{3,2,1,0:T(8,128)(2,1)}) custom-call(s32[2]{0:T(128)} %ids_v.1, s32[2]{0:T(128)} %ids_c.1, s32[1]{0:T(128)S(6)} %copy.14.count, f32[1,48]{1,0:T(1,128)} %bitcast.8, f32[1,16]{1,0:T(1,128)} %bitcast.9, s32[1,9216]{1,0:T(1,128)} %bitcast.7, s32[288,256]{1,0:T(8,128)} %constant.14.clone.keys, ...), custom_call_target="tpu_custom_call" | custom-call | tf_op jit(solution)/shard_map/pallas_call | solution.py:399
  27.9 5.5 %shard_map.128 = f32[1152,2304]{1,0:T(8,128)} custom-call(bf16[128,1152]{1,0:T(8,128)(2,1)} %bitcast.6, bf16[128,2304]{1,0:T(8,128)(2,1)} %bitcast.5), custom_call_target="tpu_custom_call" | custom-call | tf_op jit(solution)/shard_map/pallas_call | solution.py:448

commit v7 on v4

--- a/solution.py
+++ b/solution.py
@@ -356,8 +356,8 @@
     return pl.pallas_call(
         functools.partial(body, reach, short, width, layout),
         out_shape=[
-            jax.ShapeDtypeStruct((n_pair, chunks, 2 * CHUNK, col_pad), BF16),
-            jax.ShapeDtypeStruct((n_pair, chunks, 2 * CHUNK, row_pad), BF16),
+            pltpu.VMEM((n_pair, chunks, 2 * CHUNK, col_pad), BF16),
+            pltpu.VMEM((n_pair, chunks, 2 * CHUNK, row_pad), BF16),
         ],
         in_specs=[pl.BlockSpec(memory_space=pltpu.SMEM)] * len(ids) + [vmem] * len(args)
         + [pl.BlockSpec(memory_space=pl.ANY)] * len(large),
@@ -408,7 +408,7 @@
             pltpu.VMEM((n_rows, n_cols), F32),
             pltpu.SemaphoreType.DMA((pieces,)),
         ],
-        compiler_params=pltpu.CompilerParams(vmem_limit_bytes=62 * 2**20),
+        compiler_params=pltpu.CompilerParams(vmem_limit_bytes=48 * 2**20),
     )(rows, cols)
 
 

time: 33.5 us -> 31.4 us (0.937)
  Pallas kernels: 32.6 us -> 30.6 us
    pallas_call x1, Pallas kernels: 5.62 us -> 4.46 us  [product(): pl.pallas_call(functools.partial(product_kernel, scale, pieces), out_shap...]
    pallas_call x1, Pallas kernels: 27 us -> 26.1 us  [panels(): pl.pallas_call(functools.partial(body, reach, short, width, layout), out_...]
where the time goes in v7:
time: 31.4 us; the launch traced here: 31.2 us
  Pallas kernels  30.6 us (97%)
  between operations  0.66 us (2%)
    pallas_call x1, Pallas kernels, panels(): pl.pallas_call(functools.partial(body, reach, short, width, layout), out_...  26.1 us
    pallas_call x1, Pallas kernels, product(): pl.pallas_call(functools.partial(product_kernel, scale, pieces), out_shap...  4.46 us

profile of v7, /device:TPU:0, one launch (start us, length us, event | category | flops | bytes accessed | tf_op | source)
XLA Modules:
  0.0 31.2 jit_solution(1198172500689027015)
XLA Ops:
  0.7 26.1 %shard_map.127 = (bf16[4,1,32,2304]{3,2,1,0:T(8,128)(2,1)S(1)}, bf16[4,1,32,1152]{3,2,1,0:T(8,128)(2,1)S(1)}) custom-call(s32[2]{0:T(128)} %ids_v.1, s32[2]{0:T(128)} %ids_c.1, s32[1]{0:T(128)S(6)} %copy.14.count, f32[1,48]{1,0:T(1,128)} %bitcast.8, f32[1,16]{1,0:T(1,128)} %bitcast.9, s32[1,9216]{1,0:T(1,128)} %bitcast.7, s32[288,256]{1,0:T(8,128)} %constant.14.clone.keys, ...), custom_call_target="tpu_custom_call" | custom-call | tf_op jit(solution)/shard_map/pallas_call | solution.py:356
  26.8 4.5 %shard_map.128 = f32[1152,2304]{1,0:T(8,128)} custom-call(bf16[128,1152]{1,0:T(8,128)(2,1)S(1)} %bitcast.6, bf16[128,2304]{1,0:T(8,128)(2,1)S(1)} %bitcast.5), custom_call_target="tpu_custom_call" | custom-call | tf_op jit(solution)/shard_map/pallas_call | solution.py:401

commit v8 on v7

--- a/solution.py
+++ b/solution.py
@@ -71,14 +71,15 @@
 
 def body(
     reach, short, width, layout,
-    ids_v, ids_c, count, energy_v, energy_c, g_list, keys, valence_in, conduction_in, *refs,
+    ids_v, ids_c, count, energy_v_in, energy_c_in, g_list_in, keys_in, valence_in, conduction_in, *refs,
 ):
     n_pair, n_grow, n_gcol, per_device, chunks, col_at, row_at = layout
     tables_in, (cols, rows), scratch = refs[:4], refs[4:6], refs[6:]
     bands, first_h, first_l, second_h, second_l = scratch[:5]
     infos, dens_h, dens_l, even_h, even_l, odd_h, odd_l, spec, row_buf = scratch[5:14]
     tile_info = infos.at[n_grow * n_gcol]
-    load_sem, info_send, info_recv, col_send, col_recv, relay_send, relay_recv, row_send, row_recv = scratch[14:]
+    load_sem, info_send, info_recv, col_send, col_recv, relay_send, relay_recv, row_send, row_recv = scratch[14:23]
+    energy_v, energy_c, g_list, keys = scratch[23:]
     n_v, n_c = valence_in.shape[0], conduction_in.shape[0]
 
     me, grow, gcol = lax.axis_index("pair"), lax.axis_index("grow"), lax.axis_index("gcol")
@@ -100,8 +101,8 @@
         pltpu.make_async_copy(source, target, load_sem.at[n])
         for n, (source, target) in enumerate(
             zip(
-                (valence_in, conduction_in, *tables_in),
-                (bands.at[pl.ds(0, n_v)], bands.at[pl.ds(n_v, n_c)], *scratch[1:5]),
+                (valence_in, conduction_in, *tables_in, energy_v_in, energy_c_in, g_list_in, keys_in),
+                (bands.at[pl.ds(0, n_v)], bands.at[pl.ds(n_v, n_c)], *scratch[1:5], *scratch[23:]),
             )
         )
     ]
@@ -157,8 +158,8 @@
     plane = GRID * GRID
     together = CHUNK // per_device
     dot = functools.partial(jnp.dot, preferred_element_type=F32)
-    loads[0].wait()
-    loads[1].wait()
+    for n in (0, 1, 6, 7, 8, 9):
+        loads[n].wait()
 
     def transform(n, first_chunk):
         slot = lax.broadcasted_iota(jnp.int32, (CHUNK, LANES), 0)
@@ -359,7 +360,7 @@
             pltpu.VMEM((n_pair, chunks, 2 * CHUNK, col_pad), BF16),
             pltpu.VMEM((n_pair, chunks, 2 * CHUNK, row_pad), BF16),
         ],
-        in_specs=[pl.BlockSpec(memory_space=pltpu.SMEM)] * len(ids) + [vmem] * len(args)
+        in_specs=[pl.BlockSpec(memory_space=pltpu.SMEM)] * len(ids) + [pl.BlockSpec(memory_space=pl.ANY)] * len(args)
         + [pl.BlockSpec(memory_space=pl.ANY)] * len(large),
         out_specs=[vmem] * 2,
         scratch_shapes=[pltpu.VMEM((n_v + n_c, GRID**3), BF16)]
@@ -370,11 +371,12 @@
             *[pltpu.VMEM((half // 2, 2 * width), BF16)] * 4,
             pltpu.VMEM((chunks, height, width), BF16),
             pltpu.VMEM((n_pair, chunks, 2 * CHUNK, row_pad), BF16),
-            dma((len(large),)),
+            dma((len(large) + len(args),)),
             dma((n_group,)), dma((n_group,)),
             dma((n_pair // 2,)), dma((n_pair // 2,)),
             dma((n_pair // 2,)), dma((n_pair // 2,)),
             dma((n_pair,)), dma((n_pair,)),
+            *[pltpu.VMEM(x.shape, x.dtype) for x in args],
         ],
         compiler_params=pltpu.CompilerParams(
             collective_id=0, has_side_effects=True, vmem_limit_bytes=56 * 2**20

time: 31.4 us -> 31.1 us (level)
  no operation moved by 1% of the time
where the time goes in v8:
time: 31.1 us; the launch traced here: 31 us
  Pallas kernels  30.3 us (97%)
  between operations  0.66 us (2%)
    pallas_call x1, Pallas kernels, panels(): pl.pallas_call(functools.partial(body, reach, short, width, layout), out_...  25.8 us
    pallas_call x1, Pallas kernels, product(): pl.pallas_call(functools.partial(product_kernel, scale, pieces), out_shap...  4.46 us

profile of v8, /device:TPU:0, one launch (start us, length us, event | category | flops | bytes accessed | tf_op | source)
XLA Modules:
  0.0 31.0 jit_solution(6486575510347584953)
XLA Ops:
  0.7 25.8 %shard_map.127 = (bf16[4,1,32,2304]{3,2,1,0:T(8,128)(2,1)S(1)}, bf16[4,1,32,1152]{3,2,1,0:T(8,128)(2,1)S(1)}) custom-call(s32[2]{0:T(128)} %ids_v.1, s32[2]{0:T(128)} %ids_c.1, s32[1]{0:T(128)S(6)} %copy.14.count, f32[1,48]{1,0:T(1,128)} %bitcast.8, f32[1,16]{1,0:T(1,128)} %bitcast.9, s32[1,9216]{1,0:T(1,128)} %bitcast.7, ...), custom_call_target="tpu_custom_call" | custom-call | tf_op jit(solution)/shard_map/pallas_call | solution.py:357
  26.5 4.5 %shard_map.128 = f32[1152,2304]{1,0:T(8,128)} custom-call(bf16[128,1152]{1,0:T(8,128)(2,1)S(1)} %bitcast.6, bf16[128,2304]{1,0:T(8,128)(2,1)S(1)} %bitcast.5), custom_call_target="tpu_custom_call" | custom-call | tf_op jit(solution)/shard_map/pallas_call | solution.py:403
